TPU v7x, 128 devices: a whole 4x4x4 slice. The times are simulated.
128 devices in a mesh: cache: 32 (over z, y, core), rank: 4 (over x).
Axes of the slice: x: 4, y: 4, z: 4, core: 2. Of those that a mesh axis runs over, the one named last changes fastest.
Arguments:
- hist_keys: bfloat16 [512, 640, 1024], P('cache', 'rank'), may hold values from -6 to 6
- hist_values: bfloat16 [512, 640, 1024], P('cache', 'rank'), may hold values from -6 to 6
- lengths: int32 [512], P('cache'), may hold values from 1 to 640, 163840 in all
- route: int32 [512, 1], P('cache'), may hold values from 0 to 31; in each aligned block of 16 rows (0 to 15, 16 to 31, ...) no two rows name the same one
- candidates: bfloat16 [32, 32, 128, 1024], P('cache', None, 'rank'), may hold values from -6 to 6
- w_qu: bfloat16 [1024, 2048], replicated, may hold values from -0.1875 to 0.1875
- w_out: bfloat16 [1024, 1024], replicated, may hold values from -0.1875 to 0.1875
Outputs:
- ranked: bfloat16 [32, 32, 128, 1024], P('cache', None, 'rank')
Inputs may be any that keep to these rules, and one draw needn't show every extreme that they name: `route`: among the 16 users of one cache index no two name the same group.
All inputs are finite; a program needn't handle non-finite values. No bound on the sum of `lengths` on one device may be relied on, other than what follows from the above.
Results may differ from a plain program's by a relative error of at most 0.0033.
Values may be sent and summed in bfloat16 or wider, within the bound.
No kernel may reach another device: no remote copies, remote signals or barrier semaphores. Data moves between devices by JAX's collectives and lax.ppermute only.
A program may use at most 192 MiB of HBM per device.

v0:
```python
import jax
import jax.numpy as jnp
from jax import lax
from jax.sharding import PartitionSpec as P

HEADS = 8


EPS = 1e-05


def attend(query, keys, values):
    batch, cands, width = query.shape
    events = keys.shape[1]
    head_width = width // HEADS
    query_heads = query.reshape(batch, cands, HEADS, head_width)
    key_heads = keys.reshape(batch, events, HEADS, head_width)
    value_heads = values.reshape(batch, events, HEADS, head_width)
    scores = jnp.einsum(
        "bchd,brhd->bhrc", query_heads, key_heads, preferred_element_type=jnp.float32
    )
    weights = jax.nn.silu(scores * head_width ** (-0.5)).astype(jnp.bfloat16)
    mixed = jnp.einsum("bhrc,brhd->bchd", weights, value_heads, preferred_element_type=jnp.float32)
    return mixed.reshape(batch, cands, width)


def per_device(hist_keys, hist_values, lengths, route, candidates, w_qu, w_out):
    users, hist_rows, width = hist_keys.shape
    slots = candidates.shape[1]
    local_cands = candidates.shape[2]
    position = lax.axis_index("rank") * hist_rows + jnp.arange(hist_rows, dtype=jnp.int32)
    keep = (position[None, :] < lengths[:, None])[:, :, None]
    zero = jnp.zeros((), jnp.bfloat16)
    keys_kept = jnp.where(keep, hist_keys, zero)
    values_kept = jnp.where(keep, hist_values, zero)
    placing = route == jnp.arange(slots, dtype=jnp.int32)[None, :]
    features = candidates[0]
    projected = jax.nn.silu(
        jnp.dot(features.reshape(-1, width), w_qu, preferred_element_type=jnp.float32)
    )
    projected = projected.reshape(slots, local_cands, 2 * width)
    queries = projected[:, :, :width].astype(jnp.bfloat16)
    gate = projected[:, :, width:].astype(jnp.bfloat16)
    placing_half = placing.astype(jnp.bfloat16)
    packed_keys = jnp.einsum(
        "us,urd->srd", placing_half, keys_kept, preferred_element_type=jnp.float32
    ).astype(jnp.bfloat16)
    packed_values = jnp.einsum(
        "us,urd->srd", placing_half, values_kept, preferred_element_type=jnp.float32
    ).astype(jnp.bfloat16)
    arrived_keys, arrived_values = (
        lax.all_to_all(packed_keys, "cache", split_axis=0, concat_axis=0, tiled=True),
        lax.all_to_all(packed_values, "cache", split_axis=0, concat_axis=0, tiled=True),
    )
    partial_value = attend(
        lax.all_gather(queries, "rank", axis=1, tiled=True), arrived_keys, arrived_values
    )
    mixed = lax.psum_scatter(partial_value, "rank", scatter_dimension=1, tiled=True)
    centred = mixed - jnp.mean(mixed, axis=-1, keepdims=True)
    variance = jnp.mean(centred * centred, axis=-1, keepdims=True)
    normed = centred * lax.rsqrt(variance + EPS)
    gated = (normed * gate.astype(jnp.float32)).astype(jnp.bfloat16)
    output = jnp.dot(gated.reshape(-1, width), w_out, preferred_element_type=jnp.float32).reshape(
        slots, local_cands, width
    )
    ranked = (features.astype(jnp.float32) + output).astype(jnp.bfloat16)
    return ranked.reshape(1, slots, local_cands, width)


def solution(mesh):
    placed = (
        P("cache", "rank", None),
        P("cache", "rank", None),
        P("cache"),
        P("cache", None),
        P("cache", None, "rank", None),
        P(),
        P(),
    )
    return jax.shard_map(
        per_device,
        mesh=mesh,
        in_specs=placed,
        out_specs=P("cache", None, "rank", None),
        check_vma=False,
    )
```

profile of v0, /device:TPU:6, one launch (start us, length us, event | category | flops | bytes accessed | tf_op | source)
XLA Modules:
  0.0 514.6 jit_solution(15591922811080989389)
XLA Ops:
  6.5 0.0 copy-start
  6.5 0.9 broadcast_compare_fusion
  7.4 0.0 copy-start.2
  7.4 7.3 %broadcast_select_fusion = (bf16[16,160,1024]{2,1,0:T(8,128)(2,1)S(1)}, bf16[16,160,1024]{2,1,0:T(8,128)(2,1)}) fusion(bf16[16,160,1024]{2,1,0:T(8,128)(2,1)} %param.7, pred[16,160]{1,0:T(8,128)(4,1)S(1)} %broadcast_compare_fusion, bf16[16,160,1024]{2,1,0:T(8,128)(2,1)} %param.8), kind=kLoop, calls=%fused_computation.13 | loop fusion | flops 5242880 | bytes 20974080 | tf_op jit(solution)/shard_map/jit(_where)/select_n | solution.py:34
  14.7 0.0 copy-done.2
  14.7 6.1 %convolution_convert_fusion = bf16[32,160,1024]{2,0,1:T(8,128)(2,1)} fusion(bf16[16,160,1024]{2,1,0:T(8,128)(2,1)S(1)} %get-tuple-element.5, s32[16]{0:T(128)S(1)} %bitcast.47), kind=kOutput, calls=%fused_computation.9 | convolution fusion | flops 173015552 | bytes 15728704 | tf_op jit(solution)/shard_map/us,urd->srd/dot_general | solution.py:45
  20.8 13.7 %copy.31 = bf16[32,160,1024]{2,1,0:T(8,128)(2,1)} copy(bf16[32,160,1024]{2,0,1:T(8,128)(2,1)} %convolution_convert_fusion) | data formatting | bytes 20971520 | tf_op jit(solution)/shard_map/convert_element_type | solution.py:47
  34.5 8.4 %all-to-all-start.1 = ((bf16[32,160,1024]{2,1,0:T(8,128)(2,1)}), bf16[32,160,1024]{2,1,0:T(8,128)(2,1)}, u32[]{:S(2)}, u32[]{:S(2)}) async-start(bf16[32,160,1024]{2,1,0:T(8,128)(2,1)} %copy.31), calls=%async_computation.1 | async-start | bytes 20971520 | tf_op jit(solution)/shard_map/all_to_all | solution.py:52
  43.0 0.2 all-gather.2.cloned.1.call-start
  43.2 7.9 %multiply_convert_fusion.2 = bf16[1024,2048]{1,0:T(8,128)(2,1)S(1)} fusion(bf16[1024,1024]{1,0:T(8,128)(2,1)} %bitcast.49, bf16[1024,2048]{1,0:T(8,128)(2,1)} %param.12), kind=kOutput, calls=%fused_computation.8 | convolution fusion | flops 4305453056 | bytes 10485760 | tf_op jit(solution)/shard_map/dot_general | solution.py:39
  51.2 0.0 copy-start.1
  51.2 1.9 copy-done.1
  53.1 0.2 slice.10
  53.3 2.5 copy.39
  55.8 0.0 all-gather.2.cloned.1.call-update
  55.8 8.8 %convolution_convert_fusion.1 = bf16[32,160,1024]{2,0,1:T(8,128)(2,1)} fusion(bf16[16,160,1024]{2,1,0:T(8,128)(2,1)} %get-tuple-element.6, s32[16]{0:T(128)S(1)} %bitcast.48), kind=kOutput, calls=%fused_computation.10 | convolution fusion | flops 173015552 | bytes 15728704 | tf_op jit(solution)/shard_map/us,urd->srd/dot_general | solution.py:48
  64.7 15.1 %copy.29 = bf16[32,160,1024]{2,1,0:T(8,128)(2,1)} copy(bf16[32,160,1024]{2,0,1:T(8,128)(2,1)} %convolution_convert_fusion.1) | data formatting | bytes 20971520 | tf_op jit(solution)/shard_map/convert_element_type | solution.py:50
  79.8 96.0 %all-to-all-done.1 = bf16[32,160,1024]{2,1,0:T(8,128)(2,1)} async-done(((bf16[32,160,1024]{2,1,0:T(8,128)(2,1)}), bf16[32,160,1024]{2,1,0:T(8,128)(2,1)}, u32[]{:S(2)}, u32[]{:S(2)}) %all-to-all-start.1) | async-done | bytes 10485792 | tf_op jit(solution)/shard_map/all_to_all | solution.py:52
  175.7 5.0 all-to-all-start
  180.8 0.0 reduce-scatter.2.cloned.1.call-start
  180.8 0.0 all-gather.2.cloned.1.call-done
  180.8 12.3 %copy.33 = bf16[32,128,1024]{1,2,0:T(8,128)(2,1)} copy(bf16[32,128,1024]{2,0,1:T(8,128)(2,1)} %all-gather.2.cloned.1.call-done) | data formatting | bytes 16777216 | tf_op jit(solution)/shard_map/all_gather | solution.py:56
  193.2 120.4 %all-to-all-done = bf16[32,160,1024]{2,1,0:T(8,128)(2,1)} async-done(((bf16[32,160,1024]{2,1,0:T(8,128)(2,1)}), bf16[32,160,1024]{2,1,0:T(8,128)(2,1)}, u32[]{:S(2)}, u32[]{:S(2)}) %all-to-all-start) | async-done | bytes 10485792 | tf_op jit(solution)/shard_map/all_to_all | solution.py:53
  313.6 21.6 %fusion.3 = f32[32,8,128,128]{3,2,1,0:T(8,128)} fusion(bf16[32,128,8,128]{1,3,2,0:T(8,128)(2,1)} %bitcast.44, bf16[32,160,1024]{2,1,0:T(8,128)(2,1)} %all-to-all-done.1, bf16[32,160,1024]{2,1,0:T(8,128)(2,1)} %all-to-all-done), kind=kOutput, calls=%fused_computation.4 | convolution fusion | flops 2715811840 | bytes 46137344 | tf_op jit(solution)/shard_map/bhrc,brhd->bchd/dot_general | solution.py:23
  335.2 17.4 %copy.37 = f32[32,128,1024]{2,1,0:T(8,128)} copy(f32[32,128,1024]{1,2,0:T(8,128)} %bitcast.43) | data formatting | bytes 33554432 | tf_op jit(solution)/shard_map/reshape | solution.py:24
  352.6 0.0 reduce-scatter.2.cloned.1.call-update
  352.6 142.7 %reduce-scatter.2.cloned.1.call-done = f32[32,32,1024]{2,1,0:T(8,128)} async-done(((f32[32,128,1024]{2,1,0:T(8,128)}), f32[32,32,1024]{2,1,0:T(8,128)}) %reduce-scatter.2.cloned.1.call-update) | async-done | bytes 4194320 | tf_op jit(solution)/shard_map/reduce_scatter | solution.py:58
  495.4 2.4 reduce_sum.18
  497.8 2.7 multiply_reduce_fusion
  500.6 0.0 copy-done
  500.6 7.2 %fusion.15 = bf16[1,32,32,1024]{3,2,1,0:T(8,128)(2,1)} fusion(bf16[1,32,32,1024]{3,2,1,0:T(8,128)(2,1)} %param.11, bf16[1024,1024]{1,0:T(8,128)(2,1)S(1)} %copy-done, f32[32,32,1024]{2,1,0:T(8,128)} %reduce-scatter.2.cloned.1.call-done, bf16[32,32,2048]{2,1,0:T(8,128)(2,1)} %bitcast.46, f32[32,32]{1,0:T(8,128)S(1)} %add_rsqrt_fusion, ...), kind=kOutput, calls=%fused_computation.20 | convolution fusion | flops 2155872256 | bytes 12591104 | tf_op jit(solution)/shard_map/dot_general | solution.py:63
  (3 shorter events, 0.0 us)
Async XLA Ops:
  6.5 494.0 %copy-start = (bf16[1024,1024]{1,0:T(8,128)(2,1)S(1)}, bf16[1024,1024]{1,0:T(8,128)(2,1)}, u32[]{:S(2)}) copy-start(bf16[1024,1024]{1,0:T(8,128)(2,1)} %param.13) | copy-start | bytes 6291460
  7.4 7.3 %copy-start.2 = (s32[16,1]{0,1:T(1,128)S(1)}, s32[16,1]{0,1:T(1,128)}, u32[]{:S(2)}) copy-start(s32[16,1]{0,1:T(1,128)} %param.10) | copy-start | bytes 196
  34.5 141.2 %all-to-all-start.1 = ((bf16[32,160,1024]{2,1,0:T(8,128)(2,1)}), bf16[32,160,1024]{2,1,0:T(8,128)(2,1)}, u32[]{:S(2)}, u32[]{:S(2)}) async-start(bf16[32,160,1024]{2,1,0:T(8,128)(2,1)} %copy.31), calls=%async_computation.1 | async-start | bytes 20971520 | tf_op jit(solution)/shard_map/all_to_all | solution.py:52
  43.0 137.8 %all-gather.2.cloned.1.call-start = ((), (), s32[]{:S(2)}) async-start(), calls=%async_computation.3 | async-start | bytes 10485760 | tf_op jit(solution)/shard_map/all_gather | solution.py:56
  51.2 1.9 copy-start.1
  175.7 137.8 %all-to-all-start = ((bf16[32,160,1024]{2,1,0:T(8,128)(2,1)}), bf16[32,160,1024]{2,1,0:T(8,128)(2,1)}, u32[]{:S(2)}, u32[]{:S(2)}) async-start(bf16[32,160,1024]{2,1,0:T(8,128)(2,1)} %copy.29), calls=%async_computation | async-start | bytes 20971520 | tf_op jit(solution)/shard_map/all_to_all | solution.py:53
  180.8 314.6 %reduce-scatter.2.cloned.1.call-start = ((), (), s32[]{:S(2)}) async-start(), calls=%async_computation.4 | async-start | bytes 20971520 | tf_op jit(solution)/shard_map/reduce_scatter | solution.py:58
Sparse Core Ops, SparseCore 0:
  55.9 83.2 all-gather.1
  352.7 142.5 reduce-scatter.1
where the time goes:
time: 518 us; the launch traced here: 515 us
  waiting for transfers between devices  359 us (69%)
  local copies, waits for them, and re-layouts  63.2 us (12%)
  matrix products  51.6 us (10%)
  starting transfers between devices  13.7 us (3%)
  between operations  13.5 us (3%)
  other arithmetic  13.4 us (3%)
    reduce_scatter x1, waiting for transfers between devices, per_device(): lax.psum_scatter(partial_value, 'rank', scatter_dimension=1, tiled=True)  143 us
    all_to_all x1, waiting for transfers between devices, per_device(): lax.all_to_all(packed_values, 'cache', split_axis=0, concat_axis=0, tiled...  120 us
    all_to_all x1, waiting for transfers between devices, per_device(): lax.all_to_all(packed_keys, 'cache', split_axis=0, concat_axis=0, tiled=T...  96 us
    dot_general x1, matrix products, attend(): jnp.einsum('bhrc,brhd->bchd', weights, value_heads, preferred_element_typ...  21.6 us
    reshape x1, local copies, waits for them, and re-layouts, attend(): return mixed.reshape(batch, cands, width)  17.4 us
    convert_element_type x1, local copies, waits for them, and re-layouts, per_device(): packed_values = jnp.einsum('us,urd->srd', placing_half, values_kept, pref...  15.1 us
    convert_element_type x1, local copies, waits for them, and re-layouts, per_device(): packed_keys = jnp.einsum('us,urd->srd', placing_half, keys_kept, preferre...  13.7 us
    all_gather x1, local copies, waits for them, and re-layouts, per_device(): lax.all_gather(queries, 'rank', axis=1, tiled=True)  12.3 us
  transfers between devices with their start and end apart: 4, of which 3 were waited for; matrix products, arithmetic and copies ran while one was open for 9% of the time, Pallas kernels for 0%

commit v1 on v0

v1 whole, which is shorter than its diff:
```python
import jax
import jax.numpy as jnp
from jax import lax
from jax.experimental import pallas as pl
from jax.experimental.pallas import tpu as pltpu
from jax.sharding import PartitionSpec as P

HEADS = 8
EPS = 1e-05
CHUNKS = 2
VMEM_LIMIT = 48 * 1024 * 1024

F32 = jnp.float32
BF16 = jnp.bfloat16


def whole():
    return pl.BlockSpec(memory_space=pltpu.VMEM)


def params(*semantics):
    return pltpu.CompilerParams(
        dimension_semantics=semantics or None, vmem_limit_bytes=VMEM_LIMIT
    )


def pick_kernel(route_ref, arrived_ref, picked_ref):
    for i in range(picked_ref.shape[0]):
        picked_ref[i] = arrived_ref[route_ref[i]]


def pick(route, arrived, users):
    _, cands, width = arrived.shape
    return pl.pallas_call(
        pick_kernel,
        grid_spec=pltpu.PrefetchScalarGridSpec(
            num_scalar_prefetch=1, grid=(), in_specs=[whole()], out_specs=whole()
        ),
        out_shape=jax.ShapeDtypeStruct((users, cands, width), BF16),
        compiler_params=params(),
        name="pick",
    )(route, arrived)


def attend_kernel(
    lengths_ref, rank_ref, own_ref, left_ref, right_ref, far_a_ref, far_b_ref, keys_ref, values_ref,
    out_own, out_left_a, out_left_b, out_right_a, out_right_b, out_far_a, out_far_b,
):
    step, half = pl.program_id(0), pl.num_programs(0)
    events, width = keys_ref.shape[2:]
    cands = own_ref.shape[2]
    head = 128
    factor = 0.5 * head ** (-0.5)
    for side, far_ref, out_left, out_right, out_far in (
        (0, far_a_ref, out_left_a, out_right_a, out_far_a),
        (1, far_b_ref, out_left_b, out_right_b, out_far_b),
    ):
        length = lengths_ref[step + side * half]
        position = rank_ref[0] * events + lax.broadcasted_iota(jnp.int32, (events, width), 0)
        keep = jnp.where(position < length, 1.0, 0.0).astype(BF16)
        queries = jnp.concatenate(
            [own_ref[side, 0], left_ref[side, 0], right_ref[side, 0], far_ref[0]], axis=0
        )
        keys = keys_ref[side, 0]
        values = values_ref[side, 0] * keep
        for h in range(width // head):
            cols = slice(h * head, (h + 1) * head)
            scores = lax.dot_general(
                queries[:, cols], keys[:, cols], (((1,), (1,)), ((), ())), preferred_element_type=F32
            )
            scaled = scores * factor
            weights = (scaled + scaled * jnp.tanh(scaled)).astype(BF16)
            mixed = jnp.dot(weights, values[:, cols], preferred_element_type=F32).astype(BF16)
            out_own[side, 0, :, cols] = mixed[:cands]
            out_left[0, :, cols] = mixed[cands:2 * cands]
            out_right[0, :, cols] = mixed[2 * cands:3 * cands]
            out_far[0, :, cols] = mixed[3 * cands:]


def attend(lengths, rank, own, left, right, far_a, far_b, keys, values, chunk):
    users, cands, width = own.shape
    half = users // 2
    events = keys.shape[1]

    def split(x):
        return x.reshape((2, half) + x.shape[1:])

    pair = pl.BlockSpec((2, 1, cands, width), lambda i, *_: (0, i, 0, 0))
    single = pl.BlockSpec((1, cands, width), lambda i, *_: (i, 0, 0))
    cached = pl.BlockSpec((2, 1, events, width), lambda i, *_: (0, i, 0, chunk))
    small = jax.ShapeDtypeStruct((half, cands, width), BF16)
    outs = pl.pallas_call(
        attend_kernel,
        grid_spec=pltpu.PrefetchScalarGridSpec(
            num_scalar_prefetch=2,
            grid=(half,),
            in_specs=[pair, pair, pair, single, single, cached, cached],
            out_specs=[pair] + [single] * 6,
        ),
        out_shape=[jax.ShapeDtypeStruct((2, half, cands, width), BF16)] + [small] * 6,
        compiler_params=params("arbitrary"),
        name="attend",
    )(lengths, rank, split(own), split(left), split(right), far_a, far_b, split(keys), split(values))
    return [outs[0].reshape(users, cands, width)] + list(outs[1:])


def place_kernel(route_ref, own_ref, left_a, left_b, right_a, right_b, placed_ref):
    users = own_ref.shape[0]
    half = users // 2
    placed_ref[...] = jnp.zeros_like(placed_ref)
    for i in range(users):
        left, right = (left_a, right_a) if i < half else (left_b, right_b)
        j = i % half
        total = own_ref[i].astype(F32) + left[j].astype(F32) + right[j].astype(F32)
        placed_ref[route_ref[i]] = total.astype(BF16)


def place(route, own, left_a, left_b, right_a, right_b, slots):
    _, cands, width = own.shape
    return pl.pallas_call(
        place_kernel,
        grid_spec=pltpu.PrefetchScalarGridSpec(
            num_scalar_prefetch=1, grid=(), in_specs=[whole()] * 5, out_specs=whole()
        ),
        out_shape=jax.ShapeDtypeStruct((slots, cands, width), BF16),
        compiler_params=params(),
        name="place",
    )(route, own, left_a, left_b, right_a, right_b)


def finish_kernel(*refs):
    mixed_refs, (gate_ref, features_ref, w_ref, out_ref) = refs[:-4], refs[-4:]
    mixed = jnp.concatenate([m[...] for m in mixed_refs], axis=1).astype(F32)
    centred = mixed - jnp.mean(mixed, axis=-1, keepdims=True)
    variance = jnp.mean(centred * centred, axis=-1, keepdims=True)
    normed = centred * lax.rsqrt(variance + EPS)
    gated = (normed * gate_ref[...].astype(F32)).astype(BF16)
    output = jnp.dot(gated, w_ref[...], preferred_element_type=F32)
    out_ref[...] = (features_ref[...].astype(F32) + output).astype(BF16)


def finish(mixed, gate, features, w_out, steps=4):
    rows, width = features.shape
    part = mixed[0].shape[1]
    block = rows // steps
    return pl.pallas_call(
        finish_kernel,
        grid=(steps,),
        in_specs=[pl.BlockSpec((block, part), lambda i: (i, 0))] * len(mixed)
        + [pl.BlockSpec((block, width), lambda i: (i, 0))] * 2
        + [pl.BlockSpec((width, width), lambda i: (0, 0))],
        out_specs=pl.BlockSpec((block, width), lambda i: (i, 0)),
        out_shape=jax.ShapeDtypeStruct((rows, width), BF16),
        compiler_params=params("arbitrary"),
        name="finish",
    )(*mixed, gate, features, w_out)


def rotate(x, by):
    n = 4
    return lax.ppermute(x, "rank", [(i, (i + by) % n) for i in range(n)])


def exchange(x):
    return lax.all_to_all(x, "cache", split_axis=0, concat_axis=0, tiled=True)


def per_device(hist_keys, hist_values, lengths, route, candidates, w_qu, w_out):
    users, hist_rows, width = hist_keys.shape
    slots, cands = candidates.shape[1:3]
    half = users // 2
    features = candidates.reshape(slots * cands, width)
    route = route[:, 0]
    rank = lax.axis_index("rank").astype(jnp.int32).reshape(1)
    part = width // CHUNKS

    def project(columns):
        return jax.nn.silu(jnp.dot(features, columns, preferred_element_type=F32)).astype(BF16)

    arrived = []
    for c in range(CHUNKS):
        queries = project(w_qu[:, c * part:(c + 1) * part])
        arrived.append(exchange(queries.reshape(slots, cands, part)))
    gate = project(w_qu[:, width:])
    mixed = []
    for c in range(CHUNKS):
        own = pick(route, arrived[c], users)
        left, right = rotate(own, 1), rotate(own, -1)
        far_a, far_b = rotate(left[:half], 1), rotate(right[half:], -1)
        p_own, p_left_a, p_left_b, p_right_a, p_right_b, p_far_a, p_far_b = attend(
            lengths, rank, own, left, right, far_a, far_b, hist_keys, hist_values, c
        )
        via_a, via_b = rotate(p_far_a, 1), rotate(p_far_b, -1)
        from_left_b, from_right_a = rotate(p_right_b, 1), rotate(p_left_a, -1)
        from_left_a = rotate((p_right_a.astype(F32) + via_a.astype(F32)).astype(BF16), 1)
        from_right_b = rotate((p_left_b.astype(F32) + via_b.astype(F32)).astype(BF16), -1)
        placed = place(route, p_own, from_left_a, from_left_b, from_right_a, from_right_b, slots)
        mixed.append(exchange(placed).reshape(slots * cands, part))
    ranked = finish(mixed, gate, features, w_out)
    return ranked.reshape(1, slots, cands, width)


def solution(mesh):
    placed = (
        P("cache", "rank", None),
        P("cache", "rank", None),
        P("cache"),
        P("cache", None),
        P("cache", None, "rank", None),
        P(),
        P(),
    )
    return jax.shard_map(
        per_device,
        mesh=mesh,
        in_specs=placed,
        out_specs=P("cache", None, "rank", None),
        check_vma=False,
    )
```

time: 518 us -> 191 us (0.37)
  waiting for transfers between devices: 359 us -> 73.9 us
  local copies, waits for them, and re-layouts: 63.2 us -> 8.06 us
  starting transfers between devices: 13.7 us -> 54.8 us
  matrix products: 51.6 us -> 15 us
  Pallas kernels: 0 us -> 36.4 us
  between operations: 13.5 us -> 0.19 us
  other arithmetic: 13.4 us -> 1.3 us
    all_to_all x2 -> x4, waiting for transfers between devices: 216 us -> 24 us  [exchange(): return lax.all_to_all(x, 'cache', split_axis=0, concat_axis=0, tiled=True)]
    reduce_scatter x1 -> x0, waiting for transfers between devices: 143 us -> none  [per_device(): lax.psum_scatter(partial_value, 'rank', scatter_dimension=1, tiled=True)]
    ppermute x0 -> x20, waiting for transfers between devices: none -> 49.8 us  [rotate(): return lax.ppermute(x, 'rank', [(i, (i + by) % n) for i in range(n)])]
    dot_general x5 -> x3, matrix products: 51.6 us -> 15 us  [project(): jnp.dot(features, columns, preferred_element_type=F32)]
    pallas_call x0 -> x7, Pallas kernels: none -> 36.4 us  [the longest x2 24.8 us: attend(): pl.pallas_call(attend_kernel, grid_spec=pltpu.PrefetchScalarGridSpec(num_...]
    convert_element_type x2 -> x0, local copies, waits for them, and re-layouts: 28.8 us -> none  [the longest x1 15.1 us: per_device(): packed_values = jnp.einsum('us,urd->srd', placing_half, values_kept, pref...]
    ppermute x0 -> x20, starting transfers between devices: none -> 27.8 us  [rotate(): return lax.ppermute(x, 'rank', [(i, (i + by) % n) for i in range(n)])]
    reshape x1 -> x0, local copies, waits for them, and re-layouts: 17.4 us -> none  [attend(): return mixed.reshape(batch, cands, width)]
  transfers between devices with their start and end apart: 4 -> 24, of which waited for: 3 -> 12; matrix products, arithmetic and copies ran while one was open for 9% -> 7% of each run, Pallas kernels for 0% -> 16%
where the time goes in v1:
time: 191 us; the launch traced here: 190 us
  waiting for transfers between devices  73.9 us (39%)
  starting transfers between devices  54.8 us (29%)
  Pallas kernels  36.4 us (19%)
  matrix products  15 us (8%)
  local copies, waits for them, and re-layouts  8.06 us (4%)
    ppermute x20, waiting for transfers between devices, rotate(): return lax.ppermute(x, 'rank', [(i, (i + by) % n) for i in range(n)])  49.8 us
    ppermute x20, starting transfers between devices, rotate(): return lax.ppermute(x, 'rank', [(i, (i + by) % n) for i in range(n)])  27.8 us
    all_to_all x4, starting transfers between devices, exchange(): return lax.all_to_all(x, 'cache', split_axis=0, concat_axis=0, tiled=True)  27 us
    pallas_call x2, Pallas kernels, attend(): pl.pallas_call(attend_kernel, grid_spec=pltpu.PrefetchScalarGridSpec(num_...  24.8 us
    all_to_all x4, waiting for transfers between devices, exchange(): return lax.all_to_all(x, 'cache', split_axis=0, concat_axis=0, tiled=True)  24 us
    dot_general x3, matrix products, project(): jnp.dot(features, columns, preferred_element_type=F32)  15 us
    pallas_call x1, Pallas kernels, finish(): pl.pallas_call(finish_kernel, grid=(steps,), in_specs=[pl.BlockSpec((bloc...  6.9 us
    unnamed x22, local copies, waits for them, and re-layouts  5.85 us
  transfers between devices with their start and end apart: 24, of which 12 were waited for; matrix products, arithmetic and copies ran while one was open for 7% of the time, Pallas kernels for 16%

profile of v1, /device:TPU:6, one launch (start us, length us, event | category | flops | bytes accessed | tf_op | source)
XLA Modules:
  0.0 189.6 jit_solution(5806915972302490830)
XLA Ops:
  0.0 4.4 %multiply_convert_fusion.1 = bf16[1024,512]{1,0:T(8,128)(2,1)} fusion(bf16[1024,1024]{1,0:T(8,128)(2,1)} %bitcast.39, bf16[1024,2048]{1,0:T(8,128)(2,1)} %param.12), kind=kOutput, calls=%fused_computation.3 | convolution fusion | flops 1076363264 | bytes 4194304 | tf_op jit(solution)/shard_map/dot_general | solution.py:178
  4.4 8.3 %all-to-all-start.2 = ((bf16[32,32,512]{2,1,0:T(8,128)(2,1)}), bf16[32,32,512]{2,1,0:T(8,128)(2,1)S(1)}, u32[]{:S(2)}, u32[]{:S(2)}) async-start(bf16[32,32,512]{2,1,0:T(8,128)(2,1)} %bitcast.11), calls=%async_computation.2 | async-start | bytes 2097152 | tf_op jit(solution)/shard_map/all_to_all | solution.py:165
  12.7 4.4 %multiply_convert_fusion.2 = bf16[1024,512]{1,0:T(8,128)(2,1)} fusion(bf16[1024,1024]{1,0:T(8,128)(2,1)} %bitcast.40, bf16[1024,2048]{1,0:T(8,128)(2,1)} %param.12), kind=kOutput, calls=%fused_computation.4 | convolution fusion | flops 1076363264 | bytes 4194304 | tf_op jit(solution)/shard_map/dot_general | solution.py:178
  17.1 13.0 %all-to-all-done.2.arrived_ref = bf16[32,32,512]{2,1,0:T(8,128)(2,1)S(1)} async-done(((bf16[32,32,512]{2,1,0:T(8,128)(2,1)}), bf16[32,32,512]{2,1,0:T(8,128)(2,1)S(1)}, u32[]{:S(2)}, u32[]{:S(2)}) %all-to-all-start.2) | async-done | bytes 1048608 | tf_op jit(solution)/shard_map/all_to_all | solution.py:165
  30.0 4.1 %all-to-all-start = ((bf16[32,32,512]{2,1,0:T(8,128)(2,1)}), bf16[32,32,512]{2,1,0:T(8,128)(2,1)S(1)}, u32[]{:S(2)}, u32[]{:S(2)}) async-start(bf16[32,32,512]{2,1,0:T(8,128)(2,1)} %bitcast.3), calls=%async_computation | async-start | bytes 2097152 | tf_op jit(solution)/shard_map/all_to_all | solution.py:165
  35.6 2.4 %collective-permute-start.10 = (bf16[16,32,512]{2,1,0:T(8,128)(2,1)S(1)}, bf16[16,32,512]{2,1,0:T(8,128)(2,1)S(1)}, u32[]{:S(2)}, u32[]{:S(2)}) collective-permute-start(bf16[16,32,512]{2,1,0:T(8,128)(2,1)S(1)} %pick.3), channel_id=1, source_target_pairs={{0,1},{1,2},{2,3},{3,0},{4,5},{5,6},{6,7},{7,4},{8,9},{9,10},{10,1... | collective-permute-start | bytes 1572872 | tf_op jit(solution)/shard_map/ppermute | solution.py:161
  38.0 12.0 %collective-permute-done.11 = bf16[16,32,512]{2,1,0:T(8,128)(2,1)S(1)} collective-permute-done((bf16[16,32,512]{2,1,0:T(8,128)(2,1)S(1)}, bf16[16,32,512]{2,1,0:T(8,128)(2,1)S(1)}, u32[]{:S(2)}, u32[]{:S(2)}) %collective-permute-start.11) | collective-permute-done | bytes 524320 | tf_op jit(solution)/shard_map/ppermute | solution.py:161
  50.8 3.2 %collective-permute-start.12 = (bf16[8,32,512]{2,1,0:T(8,128)(2,1)}, bf16[8,32,512]{2,1,0:T(8,128)(2,1)S(1)}, u32[]{:S(2)}, u32[]{:S(2)}) collective-permute-start(bf16[8,32,512]{2,1,0:T(8,128)(2,1)} %slice.30), channel_id=1, source_target_pairs={{0,1},{1,2},{2,3},{3,0},{4,5},{5,6},{6,7},{7,4},{8,9},{9,10},{10,1... | collective-permute-start | bytes 786440 | tf_op jit(solution)/shard_map/ppermute | solution.py:161
  54.1 4.8 %collective-permute-done.13.far_b_ref = bf16[8,32,512]{2,1,0:T(8,128)(2,1)S(1)} collective-permute-done((bf16[8,32,512]{2,1,0:T(8,128)(2,1)S(1)}, bf16[8,32,512]{2,1,0:T(8,128)(2,1)S(1)}, u32[]{:S(2)}, u32[]{:S(2)}) %collective-permute-start.13) | collective-permute-done | bytes 262176 | tf_op jit(solution)/shard_map/ppermute | solution.py:161
  62.1 12.7 %attend.3 = (bf16[2,8,32,512]{3,2,1,0:T(8,128)(2,1)S(1)}, bf16[8,32,512]{2,1,0:T(8,128)(2,1)S(1)}, bf16[8,32,512]{2,1,0:T(8,128)(2,1)S(1)}, bf16[8,32,512]{2,1,0...) custom-call(s32[16]{0:T(128)S(1)} %copy-done.7, ...), custom_call_target="tpu_custom_call" | custom-call | tf_op jit(solution)/shard_map/attend/pallas_call | solution.py:92
  75.8 3.2 %collective-permute-start.14 = (bf16[8,32,512]{2,1,0:T(8,128)(2,1)}, bf16[8,32,512]{2,1,0:T(8,128)(2,1)}, u32[]{:S(2)}, u32[]{:S(2)}) collective-permute-start(bf16[8,32,512]{2,1,0:T(8,128)(2,1)} %get-tuple-element.28), channel_id=1, source_target_pairs={{0,1},{1,2},{2,3},{3,0},{4,5},{5,6},{6,7},{7,4},{8,9},{9,10},{10,1... | collective-permute-start | bytes 786440 | tf_op jit(solution)/shard_map/ppermute | solution.py:161
  79.7 3.2 %collective-permute-start = (bf16[16,32,512]{2,1,0:T(8,128)(2,1)S(1)}, bf16[16,32,512]{2,1,0:T(8,128)(2,1)S(1)}, u32[]{:S(2)}, u32[]{:S(2)}) collective-permute-start(bf16[16,32,512]{2,1,0:T(8,128)(2,1)S(1)} %pick.2), channel_id=1, source_target_pairs={{0,1},{1,2},{2,3},{3,0},{4,5},{5,6},{6,7},{7,4},{8,9},{9,10},{10,1... | collective-permute-start | bytes 1572872 | tf_op jit(solution)/shard_map/ppermute | solution.py:161
  82.9 3.2 %collective-permute-start.16 = (bf16[8,32,512]{2,1,0:T(8,128)(2,1)}, bf16[8,32,512]{2,1,0:T(8,128)(2,1)S(1)}, u32[]{:S(2)}, u32[]{:S(2)}) collective-permute-start(bf16[8,32,512]{2,1,0:T(8,128)(2,1)} %copy-done.9), channel_id=1, source_target_pairs={{0,1},{1,2},{2,3},{3,0},{4,5},{5,6},{6,7},{7,4},{8,9},{9,10},{10,1... | collective-permute-start | bytes 786440 | tf_op jit(solution)/shard_map/ppermute | solution.py:161
  87.3 14.1 %collective-permute-done.18 = bf16[8,32,512]{2,1,0:T(8,128)(2,1)S(1)} collective-permute-done((bf16[8,32,512]{2,1,0:T(8,128)(2,1)}, bf16[8,32,512]{2,1,0:T(8,128)(2,1)S(1)}, u32[]{:S(2)}, u32[]{:S(2)}) %collective-permute-start.18) | collective-permute-done | bytes 262176 | tf_op jit(solution)/shard_map/ppermute | solution.py:161
  101.5 2.1 %collective-permute-start.19 = (bf16[8,32,512]{2,1,0:T(8,128)(2,1)S(1)}, bf16[8,32,512]{2,1,0:T(8,128)(2,1)S(1)}, u32[]{:S(2)}, u32[]{:S(2)}) collective-permute-start(bf16[8,32,512]{2,1,0:T(8,128)(2,1)S(1)} %add_convert_fusion), channel_id=1, source_target_pairs={{0,3},{1,0},{2,1},{3,2},{4,7},{5,4},{6,5},{7,6},{8,11},{9,8},{10,9... | collective-permute-start | bytes 786440 | tf_op jit(solution)/shard_map/ppermute | solution.py:161
  105.0 3.2 %collective-permute-start.2 = (bf16[8,32,512]{2,1,0:T(8,128)(2,1)}, bf16[8,32,512]{2,1,0:T(8,128)(2,1)}, u32[]{:S(2)}, u32[]{:S(2)}) collective-permute-start(bf16[8,32,512]{2,1,0:T(8,128)(2,1)} %slice.28), channel_id=1, source_target_pairs={{0,1},{1,2},{2,3},{3,0},{4,5},{5,6},{6,7},{7,4},{8,9},{9,10},{10,1... | collective-permute-start | bytes 786440 | tf_op jit(solution)/shard_map/ppermute | solution.py:161
  108.3 4.0 %collective-permute-done.19.right_b = bf16[8,32,512]{2,1,0:T(8,128)(2,1)S(1)} collective-permute-done((bf16[8,32,512]{2,1,0:T(8,128)(2,1)S(1)}, bf16[8,32,512]{2,1,0:T(8,128)(2,1)S(1)}, u32[]{:S(2)}, u32[]{:S(2)}) %collective-permute-start.19) | collective-permute-done | bytes 262176 | tf_op jit(solution)/shard_map/ppermute | solution.py:161
  112.2 1.8 place.3
  114.0 7.3 %all-to-all-start.3 = ((bf16[32,32,512]{2,1,0:T(8,128)(2,1)}), bf16[32,32,512]{2,1,0:T(8,128)(2,1)S(1)}, u32[]{:S(2)}, u32[]{:S(2)}) async-start(bf16[32,32,512]{2,1,0:T(8,128)(2,1)} %place.3), calls=%async_computation.3 | async-start | bytes 2097152 | tf_op jit(solution)/shard_map/all_to_all | solution.py:165
  121.4 12.1 %attend.2 = (bf16[2,8,32,512]{3,2,1,0:T(8,128)(2,1)S(1)}, bf16[8,32,512]{2,1,0:T(8,128)(2,1)S(1)}, bf16[8,32,512]{2,1,0:T(8,128)(2,1)S(1)}, bf16[8,32,512]{2,1,0...) custom-call(s32[16]{0:T(128)S(1)} %copy-done.7, ...), custom_call_target="tpu_custom_call" | custom-call | tf_op jit(solution)/shard_map/attend/pallas_call | solution.py:92
  133.6 2.0 %collective-permute-start.8 = (bf16[8,32,512]{2,1,0:T(8,128)(2,1)S(1)}, bf16[8,32,512]{2,1,0:T(8,128)(2,1)S(1)}, u32[]{:S(2)}, u32[]{:S(2)}) collective-permute-start(bf16[8,32,512]{2,1,0:T(8,128)(2,1)S(1)} %get-tuple-element.25), channel_id=1, source_target_pairs={{0,3},{1,0},{2,1},{3,2},{4,7},{5,4},{6,5},{7,6},{8,11},{9,8},{10,9... | collective-permute-start | bytes 786440 | tf_op jit(solution)/shard_map/ppermute | solution.py:161
  137.6 5.1 %collective-permute-done.4 = bf16[8,32,512]{2,1,0:T(8,128)(2,1)S(1)} collective-permute-done((bf16[8,32,512]{2,1,0:T(8,128)(2,1)S(1)}, bf16[8,32,512]{2,1,0:T(8,128)(2,1)S(1)}, u32[]{:S(2)}, u32[]{:S(2)}) %collective-permute-start.4) | collective-permute-done | bytes 262176 | tf_op jit(solution)/shard_map/ppermute | solution.py:161
  145.0 3.3 %collective-permute-done.6.left_b = bf16[8,32,512]{2,1,0:T(8,128)(2,1)S(1)} collective-permute-done((bf16[8,32,512]{2,1,0:T(8,128)(2,1)S(1)}, bf16[8,32,512]{2,1,0:T(8,128)(2,1)S(1)}, u32[]{:S(2)}, u32[]{:S(2)}) %collective-permute-start.6) | collective-permute-done | bytes 262176 | tf_op jit(solution)/shard_map/ppermute | solution.py:161
  148.3 1.5 collective-permute-done.7.right_a
  149.8 3.5 %collective-permute-done.5.left_a = bf16[8,32,512]{2,1,0:T(8,128)(2,1)S(1)} collective-permute-done((bf16[8,32,512]{2,1,0:T(8,128)(2,1)S(1)}, bf16[8,32,512]{2,1,0:T(8,128)(2,1)S(1)}, u32[]{:S(2)}, u32[]{:S(2)}) %collective-permute-start.5) | collective-permute-done | bytes 262176 | tf_op jit(solution)/shard_map/ppermute | solution.py:161
  153.3 1.5 collective-permute-done.9.right_b
  154.8 1.8 place.2
  156.5 7.3 %all-to-all-start.1 = ((bf16[32,32,512]{2,1,0:T(8,128)(2,1)}), bf16[32,32,512]{2,1,0:T(8,128)(2,1)S(1)}, u32[]{:S(2)}, u32[]{:S(2)}) async-start(bf16[32,32,512]{2,1,0:T(8,128)(2,1)} %place.2), calls=%async_computation.1 | async-start | bytes 2097152 | tf_op jit(solution)/shard_map/all_to_all | solution.py:165
  163.8 6.3 %multiply_convert_fusion.refs_2_ = bf16[1024,1024]{1,0:T(8,128)(2,1)} fusion(bf16[1024,1024]{1,0:T(8,128)(2,1)} %bitcast.41, bf16[1024,2048]{1,0:T(8,128)(2,1)} %param.12), kind=kOutput, calls=%fused_computation | convolution fusion | flops 2152726528 | bytes 6291456 | tf_op jit(solution)/shard_map/dot_general | solution.py:178
  170.1 11.1 %all-to-all-done.1 = bf16[32,32,512]{2,1,0:T(8,128)(2,1)S(1)} async-done(((bf16[32,32,512]{2,1,0:T(8,128)(2,1)}), bf16[32,32,512]{2,1,0:T(8,128)(2,1)S(1)}, u32[]{:S(2)}, u32[]{:S(2)}) %all-to-all-start.1) | async-done | bytes 1048608 | tf_op jit(solution)/shard_map/all_to_all | solution.py:165
  181.1 1.6 copy-done
  182.7 6.9 %finish.1 = bf16[1024,1024]{1,0:T(8,128)(2,1)} custom-call(bf16[1024,512]{1,0:T(8,128)(2,1)S(1)} %bitcast.22, bf16[1024,512]{1,0:T(8,128)(2,1)S(1)} %bitcast.21, bf16[1024,1024]{1,0:T(8,128)(2,1)S(1)} %copy-done, bf16[1024,1024]{1,0:T(8,128)(2,1)} %bitcast.42, bf16[1024,1024]{1,0:T(8,128)(2,1)} %refs_4_.1), custom_call_target="tpu_custom_call" | custom-call | tf_op jit(solution)/shard_map/finish/pallas_call | solution.py:146
  (56 shorter events, 14.3 us)
Async XLA Ops:
  4.4 25.7 %all-to-all-start.2 = ((bf16[32,32,512]{2,1,0:T(8,128)(2,1)}), bf16[32,32,512]{2,1,0:T(8,128)(2,1)S(1)}, u32[]{:S(2)}, u32[]{:S(2)}) async-start(bf16[32,32,512]{2,1,0:T(8,128)(2,1)} %bitcast.11), calls=%async_computation.2 | async-start | bytes 2097152 | tf_op jit(solution)/shard_map/all_to_all | solution.py:165
  17.1 17.0 %copy-start.6 = (s32[16,1]{0,1:T(1,128)S(1)}, s32[16,1]{0,1:T(1,128)}, u32[]{:S(2)}) copy-start(s32[16,1]{0,1:T(1,128)} %param.10) | copy-start | bytes 196
  30.0 30.2 %copy-start.7 = (s32[16]{0:T(128)S(1)}, s32[16]{0:T(128)}, u32[]{:S(2)}) copy-start(s32[16]{0:T(128)} %lengths_ref.3) | copy-start | bytes 196
  30.0 49.0 %all-to-all-start = ((bf16[32,32,512]{2,1,0:T(8,128)(2,1)}), bf16[32,32,512]{2,1,0:T(8,128)(2,1)S(1)}, u32[]{:S(2)}, u32[]{:S(2)}) async-start(bf16[32,32,512]{2,1,0:T(8,128)(2,1)} %bitcast.3), calls=%async_computation | async-start | bytes 2097152 | tf_op jit(solution)/shard_map/all_to_all | solution.py:165
  34.7 15.3 %collective-permute-start.11 = (bf16[16,32,512]{2,1,0:T(8,128)(2,1)S(1)}, bf16[16,32,512]{2,1,0:T(8,128)(2,1)S(1)}, u32[]{:S(2)}, u32[]{:S(2)}) collective-permute-start(bf16[16,32,512]{2,1,0:T(8,128)(2,1)S(1)} %pick.3), channel_id=1, source_target_pairs={{0,3},{1,0},{2,1},{3,2},{4,7},{5,4},{6,5},{7,6},{8,11},{9,8},{10,9... | collective-permute-start | bytes 1572872 | tf_op jit(solution)/shard_map/ppermute | solution.py:161
  35.6 14.5 %collective-permute-start.10 = (bf16[16,32,512]{2,1,0:T(8,128)(2,1)S(1)}, bf16[16,32,512]{2,1,0:T(8,128)(2,1)S(1)}, u32[]{:S(2)}, u32[]{:S(2)}) collective-permute-start(bf16[16,32,512]{2,1,0:T(8,128)(2,1)S(1)} %pick.3), channel_id=1, source_target_pairs={{0,1},{1,2},{2,3},{3,0},{4,5},{5,6},{6,7},{7,4},{8,9},{9,10},{10,1... | collective-permute-start | bytes 1572872 | tf_op jit(solution)/shard_map/ppermute | solution.py:161
  50.0 8.8 %collective-permute-start.13 = (bf16[8,32,512]{2,1,0:T(8,128)(2,1)S(1)}, bf16[8,32,512]{2,1,0:T(8,128)(2,1)S(1)}, u32[]{:S(2)}, u32[]{:S(2)}) collective-permute-start(bf16[8,32,512]{2,1,0:T(8,128)(2,1)S(1)} %slice.31), channel_id=1, source_target_pairs={{0,3},{1,0},{2,1},{3,2},{4,7},{5,4},{6,5},{7,6},{8,11},{9,8},{10,9... | collective-permute-start | bytes 786440 | tf_op jit(solution)/shard_map/ppermute | solution.py:161
  50.8 8.7 %collective-permute-start.12 = (bf16[8,32,512]{2,1,0:T(8,128)(2,1)}, bf16[8,32,512]{2,1,0:T(8,128)(2,1)S(1)}, u32[]{:S(2)}, u32[]{:S(2)}) collective-permute-start(bf16[8,32,512]{2,1,0:T(8,128)(2,1)} %slice.30), channel_id=1, source_target_pairs={{0,1},{1,2},{2,3},{3,0},{4,5},{5,6},{6,7},{7,4},{8,9},{9,10},{10,1... | collective-permute-start | bytes 786440 | tf_op jit(solution)/shard_map/ppermute | solution.py:161
  60.2 1.0 copy-start.3
  61.2 0.9 copy-start.5
  74.9 0.8 copy-start.8
  74.9 0.9 copy-start.9
  74.9 0.9 copy-start.10
  75.8 10.3 %collective-permute-start.14 = (bf16[8,32,512]{2,1,0:T(8,128)(2,1)}, bf16[8,32,512]{2,1,0:T(8,128)(2,1)}, u32[]{:S(2)}, u32[]{:S(2)}) collective-permute-start(bf16[8,32,512]{2,1,0:T(8,128)(2,1)} %get-tuple-element.28), channel_id=1, source_target_pairs={{0,1},{1,2},{2,3},{3,0},{4,5},{5,6},{6,7},{7,4},{8,9},{9,10},{10,1... | collective-permute-start | bytes 786440 | tf_op jit(solution)/shard_map/ppermute | solution.py:161
  79.6 21.8 %collective-permute-start.1 = (bf16[16,32,512]{2,1,0:T(8,128)(2,1)S(1)}, bf16[16,32,512]{2,1,0:T(8,128)(2,1)S(1)}, u32[]{:S(2)}, u32[]{:S(2)}) collective-permute-start(bf16[16,32,512]{2,1,0:T(8,128)(2,1)S(1)} %pick.2), channel_id=1, source_target_pairs={{0,3},{1,0},{2,1},{3,2},{4,7},{5,4},{6,5},{7,6},{8,11},{9,8},{10,9... | collective-permute-start | bytes 1572872 | tf_op jit(solution)/shard_map/ppermute | solution.py:161
  79.7 24.6 %collective-permute-start = (bf16[16,32,512]{2,1,0:T(8,128)(2,1)S(1)}, bf16[16,32,512]{2,1,0:T(8,128)(2,1)S(1)}, u32[]{:S(2)}, u32[]{:S(2)}) collective-permute-start(bf16[16,32,512]{2,1,0:T(8,128)(2,1)S(1)} %pick.2), channel_id=1, source_target_pairs={{0,1},{1,2},{2,3},{3,0},{4,5},{5,6},{6,7},{7,4},{8,9},{9,10},{10,1... | collective-permute-start | bytes 1572872 | tf_op jit(solution)/shard_map/ppermute | solution.py:161
  82.9 18.5 %collective-permute-start.18 = (bf16[8,32,512]{2,1,0:T(8,128)(2,1)}, bf16[8,32,512]{2,1,0:T(8,128)(2,1)S(1)}, u32[]{:S(2)}, u32[]{:S(2)}) collective-permute-start(bf16[8,32,512]{2,1,0:T(8,128)(2,1)} %copy-done.10), channel_id=1, source_target_pairs={{0,3},{1,0},{2,1},{3,2},{4,7},{5,4},{6,5},{7,6},{8,11},{9,8},{10,9... | collective-permute-start | bytes 786440 | tf_op jit(solution)/shard_map/ppermute | solution.py:161
  82.9 22.1 %collective-permute-start.16 = (bf16[8,32,512]{2,1,0:T(8,128)(2,1)}, bf16[8,32,512]{2,1,0:T(8,128)(2,1)S(1)}, u32[]{:S(2)}, u32[]{:S(2)}) collective-permute-start(bf16[8,32,512]{2,1,0:T(8,128)(2,1)} %copy-done.9), channel_id=1, source_target_pairs={{0,1},{1,2},{2,3},{3,0},{4,5},{5,6},{6,7},{7,4},{8,9},{9,10},{10,1... | collective-permute-start | bytes 786440 | tf_op jit(solution)/shard_map/ppermute | solution.py:161
  86.2 22.1 %collective-permute-start.17 = (bf16[8,32,512]{2,1,0:T(8,128)(2,1)}, bf16[8,32,512]{2,1,0:T(8,128)(2,1)S(1)}, u32[]{:S(2)}, u32[]{:S(2)}) collective-permute-start(bf16[8,32,512]{2,1,0:T(8,128)(2,1)} %copy-done.8), channel_id=1, source_target_pairs={{0,3},{1,0},{2,1},{3,2},{4,7},{5,4},{6,5},{7,6},{8,11},{9,8},{10,9... | collective-permute-start | bytes 786440 | tf_op jit(solution)/shard_map/ppermute | solution.py:161
  101.4 6.9 %collective-permute-start.15 = (bf16[8,32,512]{2,1,0:T(8,128)(2,1)S(1)}, bf16[8,32,512]{2,1,0:T(8,128)(2,1)S(1)}, u32[]{:S(2)}, u32[]{:S(2)}) collective-permute-start(bf16[8,32,512]{2,1,0:T(8,128)(2,1)S(1)} %add_convert_fusion.1), channel_id=1, source_target_pairs={{0,1},{1,2},{2,3},{3,0},{4,5},{5,6},{6,7},{7,4},{8,9},{9,10},{10,1... | collective-permute-start | bytes 786440 | tf_op jit(solution)/shard_map/ppermute | solution.py:161
  101.5 10.8 %collective-permute-start.19 = (bf16[8,32,512]{2,1,0:T(8,128)(2,1)S(1)}, bf16[8,32,512]{2,1,0:T(8,128)(2,1)S(1)}, u32[]{:S(2)}, u32[]{:S(2)}) collective-permute-start(bf16[8,32,512]{2,1,0:T(8,128)(2,1)S(1)} %add_convert_fusion), channel_id=1, source_target_pairs={{0,3},{1,0},{2,1},{3,2},{4,7},{5,4},{6,5},{7,6},{8,11},{9,8},{10,9... | collective-permute-start | bytes 786440 | tf_op jit(solution)/shard_map/ppermute | solution.py:161
  104.3 17.1 %collective-permute-start.3 = (bf16[8,32,512]{2,1,0:T(8,128)(2,1)}, bf16[8,32,512]{2,1,0:T(8,128)(2,1)S(1)}, u32[]{:S(2)}, u32[]{:S(2)}) collective-permute-start(bf16[8,32,512]{2,1,0:T(8,128)(2,1)} %slice.29), channel_id=1, source_target_pairs={{0,3},{1,0},{2,1},{3,2},{4,7},{5,4},{6,5},{7,6},{8,11},{9,8},{10,9... | collective-permute-start | bytes 786440 | tf_op jit(solution)/shard_map/ppermute | solution.py:161
  105.0 16.3 %collective-permute-start.2 = (bf16[8,32,512]{2,1,0:T(8,128)(2,1)}, bf16[8,32,512]{2,1,0:T(8,128)(2,1)}, u32[]{:S(2)}, u32[]{:S(2)}) collective-permute-start(bf16[8,32,512]{2,1,0:T(8,128)(2,1)} %slice.28), channel_id=1, source_target_pairs={{0,1},{1,2},{2,3},{3,0},{4,5},{5,6},{6,7},{7,4},{8,9},{9,10},{10,1... | collective-permute-start | bytes 786440 | tf_op jit(solution)/shard_map/ppermute | solution.py:161
  114.0 42.5 %all-to-all-start.3 = ((bf16[32,32,512]{2,1,0:T(8,128)(2,1)}), bf16[32,32,512]{2,1,0:T(8,128)(2,1)S(1)}, u32[]{:S(2)}, u32[]{:S(2)}) async-start(bf16[32,32,512]{2,1,0:T(8,128)(2,1)} %place.3), calls=%async_computation.3 | async-start | bytes 2097152 | tf_op jit(solution)/shard_map/all_to_all | solution.py:165
  133.5 9.2 %collective-permute-start.4 = (bf16[8,32,512]{2,1,0:T(8,128)(2,1)S(1)}, bf16[8,32,512]{2,1,0:T(8,128)(2,1)S(1)}, u32[]{:S(2)}, u32[]{:S(2)}) collective-permute-start(bf16[8,32,512]{2,1,0:T(8,128)(2,1)S(1)} %get-tuple-element.21), channel_id=1, source_target_pairs={{0,1},{1,2},{2,3},{3,0},{4,5},{5,6},{6,7},{7,4},{8,9},{9,10},{10,1... | collective-permute-start | bytes 786440 | tf_op jit(solution)/shard_map/ppermute | solution.py:161
  133.6 10.6 %collective-permute-start.8 = (bf16[8,32,512]{2,1,0:T(8,128)(2,1)S(1)}, bf16[8,32,512]{2,1,0:T(8,128)(2,1)S(1)}, u32[]{:S(2)}, u32[]{:S(2)}) collective-permute-start(bf16[8,32,512]{2,1,0:T(8,128)(2,1)S(1)} %get-tuple-element.25), channel_id=1, source_target_pairs={{0,3},{1,0},{2,1},{3,2},{4,7},{5,4},{6,5},{7,6},{8,11},{9,8},{10,9... | collective-permute-start | bytes 786440 | tf_op jit(solution)/shard_map/ppermute | solution.py:161
  135.6 12.7 %collective-permute-start.6 = (bf16[8,32,512]{2,1,0:T(8,128)(2,1)S(1)}, bf16[8,32,512]{2,1,0:T(8,128)(2,1)S(1)}, u32[]{:S(2)}, u32[]{:S(2)}) collective-permute-start(bf16[8,32,512]{2,1,0:T(8,128)(2,1)S(1)} %get-tuple-element.22), channel_id=1, source_target_pairs={{0,1},{1,2},{2,3},{3,0},{4,5},{5,6},{6,7},{7,4},{8,9},{9,10},{10,1... | collective-permute-start | bytes 786440 | tf_op jit(solution)/shard_map/ppermute | solution.py:161
  137.1 12.7 %collective-permute-start.7 = (bf16[8,32,512]{2,1,0:T(8,128)(2,1)S(1)}, bf16[8,32,512]{2,1,0:T(8,128)(2,1)S(1)}, u32[]{:S(2)}, u32[]{:S(2)}) collective-permute-start(bf16[8,32,512]{2,1,0:T(8,128)(2,1)S(1)} %get-tuple-element.23), channel_id=1, source_target_pairs={{0,3},{1,0},{2,1},{3,2},{4,7},{5,4},{6,5},{7,6},{8,11},{9,8},{10,9... | collective-permute-start | bytes 786440 | tf_op jit(solution)/shard_map/ppermute | solution.py:161
  142.8 10.5 %collective-permute-start.5 = (bf16[8,32,512]{2,1,0:T(8,128)(2,1)S(1)}, bf16[8,32,512]{2,1,0:T(8,128)(2,1)S(1)}, u32[]{:S(2)}, u32[]{:S(2)}) collective-permute-start(bf16[8,32,512]{2,1,0:T(8,128)(2,1)S(1)} %add_convert_fusion.3), channel_id=1, source_target_pairs={{0,1},{1,2},{2,3},{3,0},{4,5},{5,6},{6,7},{7,4},{8,9},{9,10},{10,1... | collective-permute-start | bytes 786440 | tf_op jit(solution)/shard_map/ppermute | solution.py:161
  144.3 10.5 %collective-permute-start.9 = (bf16[8,32,512]{2,1,0:T(8,128)(2,1)S(1)}, bf16[8,32,512]{2,1,0:T(8,128)(2,1)S(1)}, u32[]{:S(2)}, u32[]{:S(2)}) collective-permute-start(bf16[8,32,512]{2,1,0:T(8,128)(2,1)S(1)} %add_convert_fusion.2), channel_id=1, source_target_pairs={{0,3},{1,0},{2,1},{3,2},{4,7},{5,4},{6,5},{7,6},{8,11},{9,8},{10,9... | collective-permute-start | bytes 786440 | tf_op jit(solution)/shard_map/ppermute | solution.py:161
  156.5 24.6 %all-to-all-start.1 = ((bf16[32,32,512]{2,1,0:T(8,128)(2,1)}), bf16[32,32,512]{2,1,0:T(8,128)(2,1)S(1)}, u32[]{:S(2)}, u32[]{:S(2)}) async-start(bf16[32,32,512]{2,1,0:T(8,128)(2,1)} %place.2), calls=%async_computation.1 | async-start | bytes 2097152 | tf_op jit(solution)/shard_map/all_to_all | solution.py:165
  181.1 1.6 copy-start
  (3 other events, 2.1 us)

commit v2 on v0

v2 whole, which is shorter than its diff:
```python
import jax
import jax.numpy as jnp
from jax import lax
from jax.experimental import pallas as pl
from jax.experimental.pallas import tpu as pltpu
from jax.sharding import PartitionSpec as P

HEADS = 8
EPS = 1e-05
MIB = 1024 * 1024
CHUNKS = 2

F32 = jnp.float32
BF16 = jnp.bfloat16


def whole():
    return pl.BlockSpec(memory_space=pltpu.VMEM)


def params(mib):
    return pltpu.CompilerParams(vmem_limit_bytes=mib * MIB)


def pick_kernel(route_ref, arrived_ref, *picked_refs):
    half, _, part = picked_refs[0].shape
    for c in range(CHUNKS):
        cols = slice(c * part, (c + 1) * part)
        for side in range(2):
            for i in range(half):
                picked_refs[2 * c + side][i] = arrived_ref[route_ref[side * half + i], :, cols]


def pick(route, arrived, users):
    _, cands, width = arrived.shape
    half = jax.ShapeDtypeStruct((users // 2, cands, width // CHUNKS), BF16)
    outs = pl.pallas_call(
        pick_kernel,
        grid_spec=pltpu.PrefetchScalarGridSpec(
            num_scalar_prefetch=1, grid=(), in_specs=[whole()], out_specs=[whole()] * 2 * CHUNKS
        ),
        out_shape=[half] * 2 * CHUNKS,
        compiler_params=params(8),
        name="pick",
    )(route, arrived)
    return [outs[2 * c:2 * c + 2] for c in range(CHUNKS)]


def attend_kernel(lengths_ref, rank_ref, *refs):
    queries_refs, (keys_ref, values_ref), outs = refs[:8], refs[8:10], refs[10:]
    step = pl.program_id(0)
    half = lengths_ref.shape[0] // 2
    group, events, width = keys_ref.shape[1:]
    cands = outs[0].shape[1]
    head = 128
    factor = 0.5 * head ** (-0.5)
    position = rank_ref[0] * events + lax.broadcasted_iota(jnp.int32, (events, head), 0)
    jobs = [(side, u, h) for side in range(2) for u in range(group) for h in range(width // head)]
    keeps = {}
    for side in range(2):
        for u in range(group):
            length = lengths_ref[side * half + step * group + u]
            keeps[side, u] = jnp.where(position < length, 1.0, 0.0).astype(BF16)
    weights = []
    for side, u, h in jobs:
        cols = slice(h * head, (h + 1) * head)
        queries = jnp.concatenate([ref[u, :, cols] for ref in queries_refs[side::2]], axis=0)
        scores = lax.dot_general(
            queries,
            keys_ref[side, u, :, cols],
            (((1,), (1,)), ((), ())),
            preferred_element_type=F32,
        )
        scaled = scores * factor
        weights.append((scaled + scaled * jnp.tanh(scaled)).astype(BF16))
    for (side, u, h), weight in zip(jobs, weights):
        cols = slice(h * head, (h + 1) * head)
        values = values_ref[side, u, :, cols] * keeps[side, u]
        mixed = jnp.dot(weight, values, preferred_element_type=F32).astype(BF16)
        for n, out in enumerate(outs[side::2]):
            out[u, :, cols] = mixed[n * cands:(n + 1) * cands]


def attend(lengths, rank, queries, keys, values, chunk, group=2):
    half, cands, width = queries[0].shape
    events = keys.shape[1]

    def split(x):
        return x.reshape((2, half) + x.shape[1:])

    single = pl.BlockSpec((group, cands, width), lambda i, *_: (i, 0, 0))
    cached = pl.BlockSpec((2, group, events, width), lambda i, *_: (0, i, 0, chunk))
    return pl.pallas_call(
        attend_kernel,
        grid_spec=pltpu.PrefetchScalarGridSpec(
            num_scalar_prefetch=2,
            grid=(half // group,),
            in_specs=[single] * 8 + [cached] * 2,
            out_specs=[single] * 8,
        ),
        out_shape=[jax.ShapeDtypeStruct((half, cands, width), BF16)] * 8,
        compiler_params=params(48),
        name="attend",
    )(lengths, rank, *queries, split(keys), split(values))


def merge_kernel(right_ref, left_ref, via_a_ref, via_b_ref, to_right_ref, to_left_ref):
    to_right_ref[...] = (right_ref[...].astype(F32) + via_a_ref[...].astype(F32)).astype(BF16)
    to_left_ref[...] = (left_ref[...].astype(F32) + via_b_ref[...].astype(F32)).astype(BF16)


def merge(right_a, left_b, via_a, via_b):
    return pl.pallas_call(
        merge_kernel,
        in_specs=[whole()] * 4,
        out_specs=[whole()] * 2,
        out_shape=[jax.ShapeDtypeStruct(via_a.shape, BF16)] * 2,
        compiler_params=params(8),
        name="merge",
    )(right_a, left_b, via_a, via_b)


def place_kernel(route_ref, *refs):
    placed_ref = refs[-1]
    half, _, part = refs[0].shape
    width = part * CHUNKS
    placed_ref[...] = jnp.zeros_like(placed_ref)
    for side in range(2):
        for i in range(half):
            slot = route_ref[side * half + i]
            mixed = []
            for c in range(CHUNKS):
                own, left, right = (ref[i].astype(F32) for ref in refs[6 * c + side:6 * c + 6:2])
                mixed.append(own + left + right)
            mean = sum(jnp.sum(m, axis=-1, keepdims=True) for m in mixed) / width
            centred = [m - mean for m in mixed]
            variance = sum(jnp.sum(m * m, axis=-1, keepdims=True) for m in centred) / width
            scale = lax.rsqrt(variance + EPS)
            for c in range(CHUNKS):
                placed_ref[slot, :, c * part:(c + 1) * part] = (centred[c] * scale).astype(BF16)


def place(route, parts, slots):
    _, cands, part = parts[0].shape
    return pl.pallas_call(
        place_kernel,
        grid_spec=pltpu.PrefetchScalarGridSpec(
            num_scalar_prefetch=1, grid=(), in_specs=[whole()] * len(parts), out_specs=whole()
        ),
        out_shape=jax.ShapeDtypeStruct((slots, cands, part * CHUNKS), BF16),
        compiler_params=params(12),
        name="place",
    )(route, *parts)


def project_kernel(features_ref, w_ref, out_ref):
    projected = jnp.dot(features_ref[...], w_ref[...], preferred_element_type=F32)
    halved = 0.5 * projected
    out_ref[...] = (halved + halved * jnp.tanh(halved)).astype(BF16)


def project(features, w_qu, first, columns, steps=4):
    rows, width = features.shape
    block = rows // steps
    return pl.pallas_call(
        project_kernel,
        grid=(steps,),
        in_specs=[
            pl.BlockSpec((block, width), lambda i: (i, 0)),
            pl.BlockSpec((width, columns), lambda i: (0, first // columns)),
        ],
        out_specs=pl.BlockSpec((block, columns), lambda i: (i, 0)),
        out_shape=jax.ShapeDtypeStruct((rows, columns), BF16),
        compiler_params=params(62),
        name="project",
    )(features, w_qu)


def finish_kernel(normed_ref, gate_ref, features_ref, w_ref, out_ref):
    gated = (normed_ref[...].astype(F32) * gate_ref[...].astype(F32)).astype(BF16)
    output = jnp.dot(gated, w_ref[...], preferred_element_type=F32)
    out_ref[...] = (features_ref[...].astype(F32) + output).astype(BF16)


def finish(normed, gate, features, w_out, steps=4):
    rows, width = features.shape
    rows_spec = pl.BlockSpec((rows // steps, width), lambda i: (i, 0))
    return pl.pallas_call(
        finish_kernel,
        grid=(steps,),
        in_specs=[rows_spec] * 3 + [pl.BlockSpec((width, width), lambda i: (0, 0))],
        out_specs=rows_spec,
        out_shape=jax.ShapeDtypeStruct((rows, width), BF16),
        compiler_params=params(62),
        name="finish",
    )(normed, gate, features, w_out)


def rotate(x, by):
    n = 4
    return lax.ppermute(x, "rank", [(i, (i + by) % n) for i in range(n)])


def exchange(x):
    return lax.all_to_all(x, "cache", split_axis=0, concat_axis=0, tiled=True)


def after(x, *others):
    return lax.optimization_barrier((x,) + others)[0]


def per_device(hist_keys, hist_values, lengths, route, candidates, w_qu, w_out):
    users, _, width = hist_keys.shape
    slots, cands = candidates.shape[1:3]
    features = candidates.reshape(slots * cands, width)
    route = route[:, 0]
    rank = lax.axis_index("rank").astype(jnp.int32).reshape(1)

    queries = project(features, w_qu, 0, width)
    arrived = exchange(queries.reshape(slots, cands, width))
    gate = project(after(features, queries), w_qu, width, width)
    own = pick(route, arrived, users)
    gathered = []
    for c in range(CHUNKS):
        own_a, own_b = own[c]
        if c > 0:
            own_a, own_b = lax.optimization_barrier((own_a, own_b, *gathered[c - 1][2:6:3]))[:2]
        left_a, left_b = rotate(own_a, 1), rotate(own_b, 1)
        right_a, right_b = rotate(own_a, -1), rotate(own_b, -1)
        far_a, far_b = rotate(left_a, 1), rotate(right_b, -1)
        gathered.append([*own[c], left_a, left_b, right_a, right_b, far_a, far_b])
    parts = []
    for c in range(CHUNKS):
        p_own_a, p_own_b, p_left_a, p_left_b, p_right_a, p_right_b, p_far_a, p_far_b = attend(
            lengths, rank, gathered[c], hist_keys, hist_values, c
        )
        via_a, via_b = rotate(p_far_a, 1), rotate(p_far_b, -1)
        from_left_b, from_right_a = rotate(p_right_b, 1), rotate(p_left_a, -1)
        to_right_a, to_left_b = merge(p_right_a, p_left_b, via_a, via_b)
        from_left_a, from_right_b = rotate(to_right_a, 1), rotate(to_left_b, -1)
        parts += [p_own_a, p_own_b, from_left_a, from_left_b, from_right_a, from_right_b]
    normed = exchange(place(route, parts, slots)).reshape(slots * cands, width)
    ranked = finish(normed, gate, features, w_out)
    return ranked.reshape(1, slots, cands, width)


def solution(mesh):
    placed = (
        P("cache", "rank", None),
        P("cache", "rank", None),
        P("cache"),
        P("cache", None),
        P("cache", None, "rank", None),
        P(),
        P(),
    )
    return jax.shard_map(
        per_device,
        mesh=mesh,
        in_specs=placed,
        out_specs=P("cache", None, "rank", None),
        check_vma=False,
    )
```

time: 518 us -> 165 us (0.32)
  waiting for transfers between devices: 359 us -> 62.1 us
  local copies, waits for them, and re-layouts: 63.2 us -> 0.01 us
  matrix products: 51.6 us -> 0 us
  blocking collectives: 0 us -> 37 us
  Pallas kernels: 0 us -> 36 us
  starting transfers between devices: 13.7 us -> 29.7 us
  between operations: 13.5 us -> 0.08 us
  other arithmetic: 13.4 us -> 0 us
    all_to_all x2 -> x1, waiting for transfers between devices: 216 us -> 23.8 us  [exchange(): return lax.all_to_all(x, 'cache', split_axis=0, concat_axis=0, tiled=True)]
    reduce_scatter x1 -> x0, waiting for transfers between devices: 143 us -> none  [per_device(): lax.psum_scatter(partial_value, 'rank', scatter_dimension=1, tiled=True)]
    dot_general x5 -> x0, matrix products: 51.6 us -> none  [the longest x1 21.6 us: attend(): jnp.einsum('bhrc,brhd->bchd', weights, value_heads, preferred_element_typ...]
    ppermute x0 -> x24, waiting for transfers between devices: none -> 38.2 us  [rotate(): return lax.ppermute(x, 'rank', [(i, (i + by) % n) for i in range(n)])]
    all_to_all x0 -> x1, blocking collectives: none -> 37 us  [exchange(): return lax.all_to_all(x, 'cache', split_axis=0, concat_axis=0, tiled=True)]
    pallas_call x0 -> x9, Pallas kernels: none -> 36 us  [the longest x2 12.9 us: attend(): pl.pallas_call(attend_kernel, grid_spec=pltpu.PrefetchScalarGridSpec(num_...]
    convert_element_type x2 -> x0, local copies, waits for them, and re-layouts: 28.8 us -> none  [the longest x1 15.1 us: per_device(): packed_values = jnp.einsum('us,urd->srd', placing_half, values_kept, pref...]
    ppermute x0 -> x24, starting transfers between devices: none -> 24.8 us  [rotate(): return lax.ppermute(x, 'rank', [(i, (i + by) % n) for i in range(n)])]
  transfers between devices with their start and end apart: 4 -> 25, of which waited for: 3 -> 17; matrix products, arithmetic and copies ran while one was open for 9% -> 0% of each run, Pallas kernels for 0% -> 12%
where the time goes in v2:
time: 165 us
  waiting for transfers between devices  62.1 us (38%)
  blocking collectives  37 us (22%)
  Pallas kernels  36 us (22%)
  starting transfers between devices  29.7 us (18%)
    ppermute x24, waiting for transfers between devices, rotate(): return lax.ppermute(x, 'rank', [(i, (i + by) % n) for i in range(n)])  38.2 us
    all_to_all x1, blocking collectives, exchange(): return lax.all_to_all(x, 'cache', split_axis=0, concat_axis=0, tiled=True)  37 us
    ppermute x24, starting transfers between devices, rotate(): return lax.ppermute(x, 'rank', [(i, (i + by) % n) for i in range(n)])  24.8 us
    all_to_all x1, waiting for transfers between devices, exchange(): return lax.all_to_all(x, 'cache', split_axis=0, concat_axis=0, tiled=True)  23.8 us
    pallas_call x2, Pallas kernels, attend(): pl.pallas_call(attend_kernel, grid_spec=pltpu.PrefetchScalarGridSpec(num_...  12.9 us
    pallas_call x2, Pallas kernels, project(): pl.pallas_call(project_kernel, grid=(steps,), in_specs=[pl.BlockSpec((blo...  12.2 us
    pallas_call x1, Pallas kernels, finish(): pl.pallas_call(finish_kernel, grid=(steps,), in_specs=[rows_spec] * 3 + [...  7.04 us
    all_to_all x1, starting transfers between devices, exchange(): return lax.all_to_all(x, 'cache', split_axis=0, concat_axis=0, tiled=True)  4.81 us
  transfers between devices with their start and end apart: 25, of which 17 were waited for; matrix products, arithmetic and copies ran while one was open for 0% of the time, Pallas kernels for 12%

profile of v2, /device:TPU:6, one launch (start us, length us, event | category | flops | bytes accessed | tf_op | source)
XLA Modules:
  0.0 164.9 jit_solution(7559007481170661030)
XLA Ops:
  0.0 6.1 %project.2 = bf16[1024,1024]{1,0:T(8,128)(2,1)} custom-call(bf16[1024,1024]{1,0:T(8,128)(2,1)} %bitcast.14, bf16[1024,2048]{1,0:T(8,128)(2,1)} %w_ref.4), custom_call_target="tpu_custom_call" | custom-call | tf_op jit(solution)/shard_map/project/pallas_call | solution.py:165
  6.1 37.0 %all_to_all.10.arrived_ref = bf16[32,32,1024]{2,1,0:T(8,128)(2,1)S(1)} all-to-all(bf16[32,32,1024]{2,1,0:T(8,128)(2,1)} %bitcast.17), channel_id=1, replica_groups=mesh['cache'=32,'rank'=4] {'cache'}, dimensions={0} | all-to-all | bytes 4194304 | tf_op jit(solution)/shard_map/all_to_all | solution.py:205
  44.3 1.6 collective-permute-start.3
  45.9 0.8 collective-permute-start.2
  46.7 2.4 %collective-permute-start.1 = (bf16[8,32,512]{2,1,0:T(8,128)(2,1)S(1)}, bf16[8,32,512]{2,1,0:T(8,128)(2,1)S(1)}, u32[]{:S(2)}, u32[]{:S(2)}) collective-permute-start(bf16[8,32,512]{2,1,0:T(8,128)(2,1)S(1)} %get-tuple-element.33.refs_1_), channel_id=1, source_target_pairs={{0,1},{1,2},{2,3},{3,0},{4,5},{5,6},{6,7},{7,4},{8,9},{9,10},{10,1... | collective-permute-start | bytes 786440 | tf_op jit(solution)/shard_map/ppermute | solution.py:201
  49.1 3.9 %collective-permute-done.refs_2_ = bf16[8,32,512]{2,1,0:T(8,128)(2,1)S(1)} collective-permute-done((bf16[8,32,512]{2,1,0:T(8,128)(2,1)S(1)}, bf16[8,32,512]{2,1,0:T(8,128)(2,1)S(1)}, u32[]{:S(2)}, u32[]{:S(2)}) %collective-permute-start) | collective-permute-done | bytes 262176 | tf_op jit(solution)/shard_map/ppermute | solution.py:201
  53.0 1.7 %collective-permute-done.3.refs_5_ = bf16[8,32,512]{2,1,0:T(8,128)(2,1)S(1)} collective-permute-done((bf16[8,32,512]{2,1,0:T(8,128)(2,1)S(1)}, bf16[8,32,512]{2,1,0:T(8,128)(2,1)S(1)}, u32[]{:S(2)}, u32[]{:S(2)}) %collective-permute-start.3) | collective-permute-done | bytes 262176 | tf_op jit(solution)/shard_map/ppermute | solution.py:201
  55.0 1.5 collective-permute-start.12
  57.0 3.3 %collective-permute-done.2.refs_4_ = bf16[8,32,512]{2,1,0:T(8,128)(2,1)S(1)} collective-permute-done((bf16[8,32,512]{2,1,0:T(8,128)(2,1)S(1)}, bf16[8,32,512]{2,1,0:T(8,128)(2,1)S(1)}, u32[]{:S(2)}, u32[]{:S(2)}) %collective-permute-start.2) | collective-permute-done | bytes 262176 | tf_op jit(solution)/shard_map/ppermute | solution.py:201
  61.5 2.7 %collective-permute-done.4.refs_6_ = bf16[8,32,512]{2,1,0:T(8,128)(2,1)S(1)} collective-permute-done((bf16[8,32,512]{2,1,0:T(8,128)(2,1)S(1)}, bf16[8,32,512]{2,1,0:T(8,128)(2,1)S(1)}, u32[]{:S(2)}, u32[]{:S(2)}) %collective-permute-start.4) | collective-permute-done | bytes 262176 | tf_op jit(solution)/shard_map/ppermute | solution.py:201
  64.2 1.7 %collective-permute-start.13 = (bf16[8,32,512]{2,1,0:T(8,128)(2,1)S(1)}, bf16[8,32,512]{2,1,0:T(8,128)(2,1)S(1)}, u32[]{:S(2)}, u32[]{:S(2)}) collective-permute-start(bf16[8,32,512]{2,1,0:T(8,128)(2,1)S(1)} %get-tuple-element.47.refs_1_), channel_id=1, source_target_pairs={{0,1},{1,2},{2,3},{3,0},{4,5},{5,6},{6,7},{7,4},{8,9},{9,10},{10,1... | collective-permute-start | bytes 786440 | tf_op jit(solution)/shard_map/ppermute | solution.py:201
  65.9 3.9 %collective-permute-done.12.refs_2_ = bf16[8,32,512]{2,1,0:T(8,128)(2,1)S(1)} collective-permute-done((bf16[8,32,512]{2,1,0:T(8,128)(2,1)S(1)}, bf16[8,32,512]{2,1,0:T(8,128)(2,1)S(1)}, u32[]{:S(2)}, u32[]{:S(2)}) %collective-permute-start.12) | collective-permute-done | bytes 262176 | tf_op jit(solution)/shard_map/ppermute | solution.py:201
  69.8 1.7 %collective-permute-start.16 = (bf16[8,32,512]{2,1,0:T(8,128)(2,1)S(1)}, bf16[8,32,512]{2,1,0:T(8,128)(2,1)}, u32[]{:S(2)}, u32[]{:S(2)}) collective-permute-start(bf16[8,32,512]{2,1,0:T(8,128)(2,1)S(1)} %collective-permute-done.12.refs_2_), channel_id=1, source_target_pairs={{0,1},{1,2},{2,3},{3,0},{4,5},{5,6},{6,7},{7,4},{8,9},{9,10},{10,1... | collective-permute-start | bytes 786440 | tf_op jit(solution)/shard_map/ppermute | solution.py:201
  72.7 6.4 %attend.2 = (bf16[8,32,512]{2,1,0:T(8,128)(2,1)S(1)}, bf16[8,32,512]{2,1,0:T(8,128)(2,1)S(1)}, bf16[8,32,512]{2,1,0:T(8,128)(2,1)S(1)}, bf16[8,32,512]{2,1,0:T(8...) custom-call(s32[16]{0:T(128)S(1)} %copy-done, ...), custom_call_target="tpu_custom_call" | custom-call | tf_op jit(solution)/shard_map/attend/pallas_call | solution.py:93
  79.1 2.2 %collective-permute-start.6 = (bf16[8,32,512]{2,1,0:T(8,128)(2,1)S(1)}, bf16[8,32,512]{2,1,0:T(8,128)(2,1)S(1)}, u32[]{:S(2)}, u32[]{:S(2)}) collective-permute-start(bf16[8,32,512]{2,1,0:T(8,128)(2,1)S(1)} %get-tuple-element.38), channel_id=1, source_target_pairs={{0,1},{1,2},{2,3},{3,0},{4,5},{5,6},{6,7},{7,4},{8,9},{9,10},{10,1... | collective-permute-start | bytes 786440 | tf_op jit(solution)/shard_map/ppermute | solution.py:201
  81.8 6.5 %attend.3 = (bf16[8,32,512]{2,1,0:T(8,128)(2,1)S(1)}, bf16[8,32,512]{2,1,0:T(8,128)(2,1)S(1)}, bf16[8,32,512]{2,1,0:T(8,128)(2,1)S(1)}, bf16[8,32,512]{2,1,0:T(8...) custom-call(s32[16]{0:T(128)S(1)} %copy-done, ...), custom_call_target="tpu_custom_call" | custom-call | tf_op jit(solution)/shard_map/attend/pallas_call | solution.py:93
  88.2 2.8 %collective-permute-start.18 = (bf16[8,32,512]{2,1,0:T(8,128)(2,1)S(1)}, bf16[8,32,512]{2,1,0:T(8,128)(2,1)S(1)}, u32[]{:S(2)}, u32[]{:S(2)}) collective-permute-start(bf16[8,32,512]{2,1,0:T(8,128)(2,1)S(1)} %get-tuple-element.52), channel_id=1, source_target_pairs={{0,1},{1,2},{2,3},{3,0},{4,5},{5,6},{6,7},{7,4},{8,9},{9,10},{10,1... | collective-permute-start | bytes 786440 | tf_op jit(solution)/shard_map/ppermute | solution.py:201
  91.1 3.2 %collective-permute-start.9 = (bf16[8,32,512]{2,1,0:T(8,128)(2,1)S(1)}, bf16[8,32,512]{2,1,0:T(8,128)(2,1)S(1)}, u32[]{:S(2)}, u32[]{:S(2)}) collective-permute-start(bf16[8,32,512]{2,1,0:T(8,128)(2,1)S(1)} %get-tuple-element.41), channel_id=1, source_target_pairs={{0,1},{1,2},{2,3},{3,0},{4,5},{5,6},{6,7},{7,4},{8,9},{9,10},{10,1... | collective-permute-start | bytes 786440 | tf_op jit(solution)/shard_map/ppermute | solution.py:201
  94.3 3.2 %collective-permute-start.21 = (bf16[8,32,512]{2,1,0:T(8,128)(2,1)S(1)}, bf16[8,32,512]{2,1,0:T(8,128)(2,1)S(1)}, u32[]{:S(2)}, u32[]{:S(2)}) collective-permute-start(bf16[8,32,512]{2,1,0:T(8,128)(2,1)S(1)} %get-tuple-element.55), channel_id=1, source_target_pairs={{0,1},{1,2},{2,3},{3,0},{4,5},{5,6},{6,7},{7,4},{8,9},{9,10},{10,1... | collective-permute-start | bytes 786440 | tf_op jit(solution)/shard_map/ppermute | solution.py:201
  98.1 3.4 %collective-permute-done.19.via_b_ref = bf16[8,32,512]{2,1,0:T(8,128)(2,1)S(1)} collective-permute-done((bf16[8,32,512]{2,1,0:T(8,128)(2,1)S(1)}, bf16[8,32,512]{2,1,0:T(8,128)(2,1)S(1)}, u32[]{:S(2)}, u32[]{:S(2)}) %collective-permute-start.19) | collective-permute-done | bytes 262176 | tf_op jit(solution)/shard_map/ppermute | solution.py:201
  101.7 1.8 %collective-permute-done.9.refs_3_ = bf16[8,32,512]{2,1,0:T(8,128)(2,1)S(1)} collective-permute-done((bf16[8,32,512]{2,1,0:T(8,128)(2,1)S(1)}, bf16[8,32,512]{2,1,0:T(8,128)(2,1)S(1)}, u32[]{:S(2)}, u32[]{:S(2)}) %collective-permute-start.9) | collective-permute-done | bytes 262176 | tf_op jit(solution)/shard_map/ppermute | solution.py:201
  103.8 3.4 %collective-permute-done.10.refs_4_ = bf16[8,32,512]{2,1,0:T(8,128)(2,1)S(1)} collective-permute-done((bf16[8,32,512]{2,1,0:T(8,128)(2,1)S(1)}, bf16[8,32,512]{2,1,0:T(8,128)(2,1)S(1)}, u32[]{:S(2)}, u32[]{:S(2)}) %collective-permute-start.10) | collective-permute-done | bytes 262176 | tf_op jit(solution)/shard_map/ppermute | solution.py:201
  107.2 1.9 %collective-permute-done.21.refs_9_ = bf16[8,32,512]{2,1,0:T(8,128)(2,1)S(1)} collective-permute-done((bf16[8,32,512]{2,1,0:T(8,128)(2,1)S(1)}, bf16[8,32,512]{2,1,0:T(8,128)(2,1)S(1)}, u32[]{:S(2)}, u32[]{:S(2)}) %collective-permute-start.21) | collective-permute-done | bytes 262176 | tf_op jit(solution)/shard_map/ppermute | solution.py:201
  109.3 3.4 %collective-permute-done.22.refs_10_ = bf16[8,32,512]{2,1,0:T(8,128)(2,1)S(1)} collective-permute-done((bf16[8,32,512]{2,1,0:T(8,128)(2,1)S(1)}, bf16[8,32,512]{2,1,0:T(8,128)(2,1)S(1)}, u32[]{:S(2)}, u32[]{:S(2)}) %collective-permute-start.22) | collective-permute-done | bytes 262176 | tf_op jit(solution)/shard_map/ppermute | solution.py:201
  112.8 1.4 collective-permute-done.8.refs_2_
  114.2 3.1 %collective-permute-done.11.refs_5_ = bf16[8,32,512]{2,1,0:T(8,128)(2,1)S(1)} collective-permute-done((bf16[8,32,512]{2,1,0:T(8,128)(2,1)S(1)}, bf16[8,32,512]{2,1,0:T(8,128)(2,1)S(1)}, u32[]{:S(2)}, u32[]{:S(2)}) %collective-permute-start.11) | collective-permute-done | bytes 262176 | tf_op jit(solution)/shard_map/ppermute | solution.py:201
  117.2 2.8 %collective-permute-done.23.refs_11_ = bf16[8,32,512]{2,1,0:T(8,128)(2,1)S(1)} collective-permute-done((bf16[8,32,512]{2,1,0:T(8,128)(2,1)S(1)}, bf16[8,32,512]{2,1,0:T(8,128)(2,1)S(1)}, u32[]{:S(2)}, u32[]{:S(2)}) %collective-permute-start.23) | collective-permute-done | bytes 262176 | tf_op jit(solution)/shard_map/ppermute | solution.py:201
  120.0 3.0 %place.1 = bf16[32,32,1024]{2,1,0:T(8,128)(2,1)} custom-call(s32[16]{0:T(128)S(1)} %bitcast.9, bf16[8,32,512]{2,1,0:T(8,128)(2,1)S(1)} %get-tuple-element.34.refs_0_, bf16[8,32,512]{2,1,0:T(8,128)(2,1)S(1)} %get-tuple-element.35.refs_1_, bf16[8,32,512]{2,1,0:T(8,128)(2,1)S(1)} %collective-permute-done.8.refs_2_, ...), custom_call_target="tpu_custom_call" | custom-call | tf_op jit(solution)/shard_map/place/pallas_call | solution.py:145
  123.0 4.8 %all-to-all-start.1 = ((bf16[32,32,1024]{2,1,0:T(8,128)(2,1)}), bf16[32,32,1024]{2,1,0:T(8,128)(2,1)}, u32[]{:S(2)}, u32[]{:S(2)}) async-start(bf16[32,32,1024]{2,1,0:T(8,128)(2,1)} %place.1), calls=%async_computation.1 | async-start | bytes 4194304 | tf_op jit(solution)/shard_map/all_to_all | solution.py:205
  127.9 6.1 %project.3.gate_ref = bf16[1024,1024]{1,0:T(8,128)(2,1)} custom-call(bf16[1024,1024]{1,0:T(8,128)(2,1)} %bitcast.15, bf16[1024,2048]{1,0:T(8,128)(2,1)} %w_ref.4), custom_call_target="tpu_custom_call" | custom-call | tf_op jit(solution)/shard_map/project/pallas_call | solution.py:165
  134.0 23.8 %all-to-all-done.1 = bf16[32,32,1024]{2,1,0:T(8,128)(2,1)} async-done(((bf16[32,32,1024]{2,1,0:T(8,128)(2,1)}), bf16[32,32,1024]{2,1,0:T(8,128)(2,1)}, u32[]{:S(2)}, u32[]{:S(2)}) %all-to-all-start.1) | async-done | bytes 2097184 | tf_op jit(solution)/shard_map/all_to_all | solution.py:205
  157.8 7.0 %finish.1 = bf16[1024,1024]{1,0:T(8,128)(2,1)} custom-call(bf16[1024,1024]{1,0:T(8,128)(2,1)} %bitcast.6.normed_ref, bf16[1024,1024]{1,0:T(8,128)(2,1)} %project.3.gate_ref, bf16[1024,1024]{1,0:T(8,128)(2,1)} %bitcast.16, bf16[1024,1024]{1,0:T(8,128)(2,1)} %w_ref.5), custom_call_target="tpu_custom_call" | custom-call | tf_op jit(solution)/shard_map/finish/pallas_call | solution.py:188
  (32 shorter events, 6.0 us)
Async XLA Ops:
  6.1 37.0 %copy-start.1 = (s32[16,1]{0,1:T(1,128)S(1)}, s32[16,1]{0,1:T(1,128)}, u32[]{:S(2)}) copy-start(s32[16,1]{0,1:T(1,128)} %param.10) | copy-start | bytes 196
  43.1 29.5 %copy-start = (s32[16]{0:T(128)S(1)}, s32[16]{0:T(128)}, u32[]{:S(2)}) copy-start(s32[16]{0:T(128)} %lengths_ref.3) | copy-start | bytes 196
  43.8 9.2 %collective-permute-start = (bf16[8,32,512]{2,1,0:T(8,128)(2,1)S(1)}, bf16[8,32,512]{2,1,0:T(8,128)(2,1)S(1)}, u32[]{:S(2)}, u32[]{:S(2)}) collective-permute-start(bf16[8,32,512]{2,1,0:T(8,128)(2,1)S(1)} %get-tuple-element.32.refs_0_), channel_id=1, source_target_pairs={{0,1},{1,2},{2,3},{3,0},{4,5},{5,6},{6,7},{7,4},{8,9},{9,10},{10,1... | collective-permute-start | bytes 786440 | tf_op jit(solution)/shard_map/ppermute | solution.py:201
  44.3 10.4 %collective-permute-start.3 = (bf16[8,32,512]{2,1,0:T(8,128)(2,1)S(1)}, bf16[8,32,512]{2,1,0:T(8,128)(2,1)S(1)}, u32[]{:S(2)}, u32[]{:S(2)}) collective-permute-start(bf16[8,32,512]{2,1,0:T(8,128)(2,1)S(1)} %get-tuple-element.33.refs_1_), channel_id=1, source_target_pairs={{0,3},{1,0},{2,1},{3,2},{4,7},{5,4},{6,5},{7,6},{8,11},{9,8},{10,9... | collective-permute-start | bytes 786440 | tf_op jit(solution)/shard_map/ppermute | solution.py:201
  45.9 14.4 %collective-permute-start.2 = (bf16[8,32,512]{2,1,0:T(8,128)(2,1)S(1)}, bf16[8,32,512]{2,1,0:T(8,128)(2,1)S(1)}, u32[]{:S(2)}, u32[]{:S(2)}) collective-permute-start(bf16[8,32,512]{2,1,0:T(8,128)(2,1)S(1)} %get-tuple-element.32.refs_0_), channel_id=1, source_target_pairs={{0,3},{1,0},{2,1},{3,2},{4,7},{5,4},{6,5},{7,6},{8,11},{9,8},{10,9... | collective-permute-start | bytes 786440 | tf_op jit(solution)/shard_map/ppermute | solution.py:201
  46.7 14.0 %collective-permute-start.1 = (bf16[8,32,512]{2,1,0:T(8,128)(2,1)S(1)}, bf16[8,32,512]{2,1,0:T(8,128)(2,1)S(1)}, u32[]{:S(2)}, u32[]{:S(2)}) collective-permute-start(bf16[8,32,512]{2,1,0:T(8,128)(2,1)S(1)} %get-tuple-element.33.refs_1_), channel_id=1, source_target_pairs={{0,1},{1,2},{2,3},{3,0},{4,5},{5,6},{6,7},{7,4},{8,9},{9,10},{10,1... | collective-permute-start | bytes 786440 | tf_op jit(solution)/shard_map/ppermute | solution.py:201
  54.7 9.5 %collective-permute-start.4 = (bf16[8,32,512]{2,1,0:T(8,128)(2,1)S(1)}, bf16[8,32,512]{2,1,0:T(8,128)(2,1)S(1)}, u32[]{:S(2)}, u32[]{:S(2)}) collective-permute-start(bf16[8,32,512]{2,1,0:T(8,128)(2,1)S(1)} %collective-permute-done.refs_2_), channel_id=1, source_target_pairs={{0,1},{1,2},{2,3},{3,0},{4,5},{5,6},{6,7},{7,4},{8,9},{9,10},{10,1... | collective-permute-start | bytes 786440 | tf_op jit(solution)/shard_map/ppermute | solution.py:201
  55.0 14.8 %collective-permute-start.12 = (bf16[8,32,512]{2,1,0:T(8,128)(2,1)S(1)}, bf16[8,32,512]{2,1,0:T(8,128)(2,1)S(1)}, u32[]{:S(2)}, u32[]{:S(2)}) collective-permute-start(bf16[8,32,512]{2,1,0:T(8,128)(2,1)S(1)} %get-tuple-element.46.refs_0_), channel_id=1, source_target_pairs={{0,1},{1,2},{2,3},{3,0},{4,5},{5,6},{6,7},{7,4},{8,9},{9,10},{10,1... | collective-permute-start | bytes 786440 | tf_op jit(solution)/shard_map/ppermute | solution.py:201
  56.5 15.0 %collective-permute-start.15 = (bf16[8,32,512]{2,1,0:T(8,128)(2,1)S(1)}, bf16[8,32,512]{2,1,0:T(8,128)(2,1)S(1)}, u32[]{:S(2)}, u32[]{:S(2)}) collective-permute-start(bf16[8,32,512]{2,1,0:T(8,128)(2,1)S(1)} %get-tuple-element.47.refs_1_), channel_id=1, source_target_pairs={{0,3},{1,0},{2,1},{3,2},{4,7},{5,4},{6,5},{7,6},{8,11},{9,8},{10,9... | collective-permute-start | bytes 786440 | tf_op jit(solution)/shard_map/ppermute | solution.py:201
  60.3 12.3 %collective-permute-start.5 = (bf16[8,32,512]{2,1,0:T(8,128)(2,1)S(1)}, bf16[8,32,512]{2,1,0:T(8,128)(2,1)}, u32[]{:S(2)}, u32[]{:S(2)}) collective-permute-start(bf16[8,32,512]{2,1,0:T(8,128)(2,1)S(1)} %collective-permute-done.3.refs_5_), channel_id=1, source_target_pairs={{0,3},{1,0},{2,1},{3,2},{4,7},{5,4},{6,5},{7,6},{8,11},{9,8},{10,9... | collective-permute-start | bytes 786440 | tf_op jit(solution)/shard_map/ppermute | solution.py:201
  60.7 20.6 %collective-permute-start.14 = (bf16[8,32,512]{2,1,0:T(8,128)(2,1)S(1)}, bf16[8,32,512]{2,1,0:T(8,128)(2,1)S(1)}, u32[]{:S(2)}, u32[]{:S(2)}) collective-permute-start(bf16[8,32,512]{2,1,0:T(8,128)(2,1)S(1)} %get-tuple-element.46.refs_0_), channel_id=1, source_target_pairs={{0,3},{1,0},{2,1},{3,2},{4,7},{5,4},{6,5},{7,6},{8,11},{9,8},{10,9... | collective-permute-start | bytes 786440 | tf_op jit(solution)/shard_map/ppermute | solution.py:201
  64.2 17.0 %collective-permute-start.13 = (bf16[8,32,512]{2,1,0:T(8,128)(2,1)S(1)}, bf16[8,32,512]{2,1,0:T(8,128)(2,1)S(1)}, u32[]{:S(2)}, u32[]{:S(2)}) collective-permute-start(bf16[8,32,512]{2,1,0:T(8,128)(2,1)S(1)} %get-tuple-element.47.refs_1_), channel_id=1, source_target_pairs={{0,1},{1,2},{2,3},{3,0},{4,5},{5,6},{6,7},{7,4},{8,9},{9,10},{10,1... | collective-permute-start | bytes 786440 | tf_op jit(solution)/shard_map/ppermute | solution.py:201
  69.8 11.4 %collective-permute-start.16 = (bf16[8,32,512]{2,1,0:T(8,128)(2,1)S(1)}, bf16[8,32,512]{2,1,0:T(8,128)(2,1)}, u32[]{:S(2)}, u32[]{:S(2)}) collective-permute-start(bf16[8,32,512]{2,1,0:T(8,128)(2,1)S(1)} %collective-permute-done.12.refs_2_), channel_id=1, source_target_pairs={{0,1},{1,2},{2,3},{3,0},{4,5},{5,6},{6,7},{7,4},{8,9},{9,10},{10,1... | collective-permute-start | bytes 786440 | tf_op jit(solution)/shard_map/ppermute | solution.py:201
  71.5 10.2 %collective-permute-start.17 = (bf16[8,32,512]{2,1,0:T(8,128)(2,1)S(1)}, bf16[8,32,512]{2,1,0:T(8,128)(2,1)}, u32[]{:S(2)}, u32[]{:S(2)}) collective-permute-start(bf16[8,32,512]{2,1,0:T(8,128)(2,1)S(1)} %collective-permute-done.15.refs_5_), channel_id=1, source_target_pairs={{0,3},{1,0},{2,1},{3,2},{4,7},{5,4},{6,5},{7,6},{8,11},{9,8},{10,9... | collective-permute-start | bytes 786440 | tf_op jit(solution)/shard_map/ppermute | solution.py:201
  79.1 15.2 %collective-permute-start.6 = (bf16[8,32,512]{2,1,0:T(8,128)(2,1)S(1)}, bf16[8,32,512]{2,1,0:T(8,128)(2,1)S(1)}, u32[]{:S(2)}, u32[]{:S(2)}) collective-permute-start(bf16[8,32,512]{2,1,0:T(8,128)(2,1)S(1)} %get-tuple-element.38), channel_id=1, source_target_pairs={{0,1},{1,2},{2,3},{3,0},{4,5},{5,6},{6,7},{7,4},{8,9},{9,10},{10,1... | collective-permute-start | bytes 786440 | tf_op jit(solution)/shard_map/ppermute | solution.py:201
  81.3 13.1 %collective-permute-start.7 = (bf16[8,32,512]{2,1,0:T(8,128)(2,1)S(1)}, bf16[8,32,512]{2,1,0:T(8,128)(2,1)S(1)}, u32[]{:S(2)}, u32[]{:S(2)}) collective-permute-start(bf16[8,32,512]{2,1,0:T(8,128)(2,1)S(1)} %get-tuple-element.39), channel_id=1, source_target_pairs={{0,3},{1,0},{2,1},{3,2},{4,7},{5,4},{6,5},{7,6},{8,11},{9,8},{10,9... | collective-permute-start | bytes 786440 | tf_op jit(solution)/shard_map/ppermute | solution.py:201
  88.2 9.6 %collective-permute-start.18 = (bf16[8,32,512]{2,1,0:T(8,128)(2,1)S(1)}, bf16[8,32,512]{2,1,0:T(8,128)(2,1)S(1)}, u32[]{:S(2)}, u32[]{:S(2)}) collective-permute-start(bf16[8,32,512]{2,1,0:T(8,128)(2,1)S(1)} %get-tuple-element.52), channel_id=1, source_target_pairs={{0,1},{1,2},{2,3},{3,0},{4,5},{5,6},{6,7},{7,4},{8,9},{9,10},{10,1... | collective-permute-start | bytes 786440 | tf_op jit(solution)/shard_map/ppermute | solution.py:201
  91.1 10.5 %collective-permute-start.19 = (bf16[8,32,512]{2,1,0:T(8,128)(2,1)S(1)}, bf16[8,32,512]{2,1,0:T(8,128)(2,1)S(1)}, u32[]{:S(2)}, u32[]{:S(2)}) collective-permute-start(bf16[8,32,512]{2,1,0:T(8,128)(2,1)S(1)} %get-tuple-element.53), channel_id=1, source_target_pairs={{0,3},{1,0},{2,1},{3,2},{4,7},{5,4},{6,5},{7,6},{8,11},{9,8},{10,9... | collective-permute-start | bytes 786440 | tf_op jit(solution)/shard_map/ppermute | solution.py:201
  91.1 12.4 %collective-permute-start.9 = (bf16[8,32,512]{2,1,0:T(8,128)(2,1)S(1)}, bf16[8,32,512]{2,1,0:T(8,128)(2,1)S(1)}, u32[]{:S(2)}, u32[]{:S(2)}) collective-permute-start(bf16[8,32,512]{2,1,0:T(8,128)(2,1)S(1)} %get-tuple-element.41), channel_id=1, source_target_pairs={{0,1},{1,2},{2,3},{3,0},{4,5},{5,6},{6,7},{7,4},{8,9},{9,10},{10,1... | collective-permute-start | bytes 786440 | tf_op jit(solution)/shard_map/ppermute | solution.py:201
  94.3 12.8 %collective-permute-start.10 = (bf16[8,32,512]{2,1,0:T(8,128)(2,1)S(1)}, bf16[8,32,512]{2,1,0:T(8,128)(2,1)S(1)}, u32[]{:S(2)}, u32[]{:S(2)}) collective-permute-start(bf16[8,32,512]{2,1,0:T(8,128)(2,1)S(1)} %get-tuple-element.42), channel_id=1, source_target_pairs={{0,3},{1,0},{2,1},{3,2},{4,7},{5,4},{6,5},{7,6},{8,11},{9,8},{10,9... | collective-permute-start | bytes 786440 | tf_op jit(solution)/shard_map/ppermute | solution.py:201
  94.3 14.7 %collective-permute-start.21 = (bf16[8,32,512]{2,1,0:T(8,128)(2,1)S(1)}, bf16[8,32,512]{2,1,0:T(8,128)(2,1)S(1)}, u32[]{:S(2)}, u32[]{:S(2)}) collective-permute-start(bf16[8,32,512]{2,1,0:T(8,128)(2,1)S(1)} %get-tuple-element.55), channel_id=1, source_target_pairs={{0,1},{1,2},{2,3},{3,0},{4,5},{5,6},{6,7},{7,4},{8,9},{9,10},{10,1... | collective-permute-start | bytes 786440 | tf_op jit(solution)/shard_map/ppermute | solution.py:201
  97.8 14.9 %collective-permute-start.22 = (bf16[8,32,512]{2,1,0:T(8,128)(2,1)S(1)}, bf16[8,32,512]{2,1,0:T(8,128)(2,1)S(1)}, u32[]{:S(2)}, u32[]{:S(2)}) collective-permute-start(bf16[8,32,512]{2,1,0:T(8,128)(2,1)S(1)} %get-tuple-element.56), channel_id=1, source_target_pairs={{0,3},{1,0},{2,1},{3,2},{4,7},{5,4},{6,5},{7,6},{8,11},{9,8},{10,9... | collective-permute-start | bytes 786440 | tf_op jit(solution)/shard_map/ppermute | solution.py:201
  101.5 12.6 %collective-permute-start.8 = (bf16[8,32,512]{2,1,0:T(8,128)(2,1)S(1)}, bf16[8,32,512]{2,1,0:T(8,128)(2,1)S(1)}, u32[]{:S(2)}, u32[]{:S(2)}) collective-permute-start(bf16[8,32,512]{2,1,0:T(8,128)(2,1)S(1)} %get-tuple-element.40), channel_id=1, source_target_pairs={{0,1},{1,2},{2,3},{3,0},{4,5},{5,6},{6,7},{7,4},{8,9},{9,10},{10,1... | collective-permute-start | bytes 786440 | tf_op jit(solution)/shard_map/ppermute | solution.py:201
  103.5 13.7 %collective-permute-start.11 = (bf16[8,32,512]{2,1,0:T(8,128)(2,1)S(1)}, bf16[8,32,512]{2,1,0:T(8,128)(2,1)S(1)}, u32[]{:S(2)}, u32[]{:S(2)}) collective-permute-start(bf16[8,32,512]{2,1,0:T(8,128)(2,1)S(1)} %get-tuple-element.43), channel_id=1, source_target_pairs={{0,3},{1,0},{2,1},{3,2},{4,7},{5,4},{6,5},{7,6},{8,11},{9,8},{10,9... | collective-permute-start | bytes 786440 | tf_op jit(solution)/shard_map/ppermute | solution.py:201
  107.2 10.1 %collective-permute-start.20 = (bf16[8,32,512]{2,1,0:T(8,128)(2,1)S(1)}, bf16[8,32,512]{2,1,0:T(8,128)(2,1)S(1)}, u32[]{:S(2)}, u32[]{:S(2)}) collective-permute-start(bf16[8,32,512]{2,1,0:T(8,128)(2,1)S(1)} %get-tuple-element.54), channel_id=1, source_target_pairs={{0,1},{1,2},{2,3},{3,0},{4,5},{5,6},{6,7},{7,4},{8,9},{9,10},{10,1... | collective-permute-start | bytes 786440 | tf_op jit(solution)/shard_map/ppermute | solution.py:201
  109.1 10.9 %collective-permute-start.23 = (bf16[8,32,512]{2,1,0:T(8,128)(2,1)S(1)}, bf16[8,32,512]{2,1,0:T(8,128)(2,1)S(1)}, u32[]{:S(2)}, u32[]{:S(2)}) collective-permute-start(bf16[8,32,512]{2,1,0:T(8,128)(2,1)S(1)} %get-tuple-element.57), channel_id=1, source_target_pairs={{0,3},{1,0},{2,1},{3,2},{4,7},{5,4},{6,5},{7,6},{8,11},{9,8},{10,9... | collective-permute-start | bytes 786440 | tf_op jit(solution)/shard_map/ppermute | solution.py:201
  123.0 34.8 %all-to-all-start.1 = ((bf16[32,32,1024]{2,1,0:T(8,128)(2,1)}), bf16[32,32,1024]{2,1,0:T(8,128)(2,1)}, u32[]{:S(2)}, u32[]{:S(2)}) async-start(bf16[32,32,1024]{2,1,0:T(8,128)(2,1)} %place.1), calls=%async_computation.1 | async-start | bytes 4194304 | tf_op jit(solution)/shard_map/all_to_all | solution.py:205

commit v3 on v2

--- a/solution.py
+++ b/solution.py
@@ -23,35 +23,37 @@
 
 
 def pick_kernel(route_ref, arrived_ref, *picked_refs):
-    half, _, part = picked_refs[0].shape
-    for c in range(CHUNKS):
-        cols = slice(c * part, (c + 1) * part)
-        for side in range(2):
-            for i in range(half):
-                picked_refs[2 * c + side][i] = arrived_ref[route_ref[side * half + i], :, cols]
+    half = picked_refs[0].shape[0]
+    for side in range(2):
+        for i in range(half):
+            picked_refs[side][i] = arrived_ref[route_ref[side * half + i]]
 
 
 def pick(route, arrived, users):
     _, cands, width = arrived.shape
-    half = jax.ShapeDtypeStruct((users // 2, cands, width // CHUNKS), BF16)
-    outs = pl.pallas_call(
+    half = jax.ShapeDtypeStruct((users // 2, cands, width), BF16)
+    return pl.pallas_call(
         pick_kernel,
         grid_spec=pltpu.PrefetchScalarGridSpec(
-            num_scalar_prefetch=1, grid=(), in_specs=[whole()], out_specs=[whole()] * 2 * CHUNKS
+            num_scalar_prefetch=1, grid=(), in_specs=[whole()], out_specs=[whole()] * 2
         ),
-        out_shape=[half] * 2 * CHUNKS,
+        out_shape=[half] * 2,
         compiler_params=params(8),
         name="pick",
     )(route, arrived)
-    return [outs[2 * c:2 * c + 2] for c in range(CHUNKS)]
 
 
 def attend_kernel(lengths_ref, rank_ref, *refs):
-    queries_refs, (keys_ref, values_ref), outs = refs[:8], refs[8:10], refs[10:]
+    queries_refs, (keys_ref, values_ref) = refs[:8], refs[8:10]
+    own_a, own_b, go_right, go_left, right_a, left_b = refs[10:]
+    outs = (
+        (own_a, go_left.at[1], right_a, go_right.at[0]),
+        (own_b, left_b, go_right.at[1], go_left.at[0]),
+    )
     step = pl.program_id(0)
     half = lengths_ref.shape[0] // 2
     group, events, width = keys_ref.shape[1:]
-    cands = outs[0].shape[1]
+    cands = own_a.shape[1]
     head = 128
     factor = 0.5 * head ** (-0.5)
     position = rank_ref[0] * events + lax.broadcasted_iota(jnp.int32, (events, head), 0)
@@ -77,7 +79,7 @@
         cols = slice(h * head, (h + 1) * head)
         values = values_ref[side, u, :, cols] * keeps[side, u]
         mixed = jnp.dot(weight, values, preferred_element_type=F32).astype(BF16)
-        for n, out in enumerate(outs[side::2]):
+        for n, out in enumerate(outs[side]):
             out[u, :, cols] = mixed[n * cands:(n + 1) * cands]
 
 
@@ -89,6 +91,9 @@
         return x.reshape((2, half) + x.shape[1:])
 
     single = pl.BlockSpec((group, cands, width), lambda i, *_: (i, 0, 0))
+    double = pl.BlockSpec((2, group, cands, width), lambda i, *_: (0, i, 0, 0))
+    small = jax.ShapeDtypeStruct((half, cands, width), BF16)
+    large = jax.ShapeDtypeStruct((2, half, cands, width), BF16)
     cached = pl.BlockSpec((2, group, events, width), lambda i, *_: (0, i, 0, chunk))
     return pl.pallas_call(
         attend_kernel,
@@ -96,28 +101,28 @@
             num_scalar_prefetch=2,
             grid=(half // group,),
             in_specs=[single] * 8 + [cached] * 2,
-            out_specs=[single] * 8,
+            out_specs=[single] * 2 + [double] * 2 + [single] * 2,
         ),
-        out_shape=[jax.ShapeDtypeStruct((half, cands, width), BF16)] * 8,
+        out_shape=[small] * 2 + [large] * 2 + [small] * 2,
         compiler_params=params(48),
         name="attend",
     )(lengths, rank, *queries, split(keys), split(values))
 
 
-def merge_kernel(right_ref, left_ref, via_a_ref, via_b_ref, to_right_ref, to_left_ref):
-    to_right_ref[...] = (right_ref[...].astype(F32) + via_a_ref[...].astype(F32)).astype(BF16)
-    to_left_ref[...] = (left_ref[...].astype(F32) + via_b_ref[...].astype(F32)).astype(BF16)
-
-
-def merge(right_a, left_b, via_a, via_b):
+def merge_kernel(right_ref, left_ref, from_left_ref, from_right_ref, to_right_ref, to_left_ref):
+    to_right_ref[...] = (right_ref[...].astype(F32) + from_left_ref[0].astype(F32)).astype(BF16)
+    to_left_ref[...] = (left_ref[...].astype(F32) + from_right_ref[0].astype(F32)).astype(BF16)
+
+
+def merge(right_a, left_b, from_left, from_right):
     return pl.pallas_call(
         merge_kernel,
         in_specs=[whole()] * 4,
         out_specs=[whole()] * 2,
-        out_shape=[jax.ShapeDtypeStruct(via_a.shape, BF16)] * 2,
+        out_shape=[jax.ShapeDtypeStruct(right_a.shape, BF16)] * 2,
         compiler_params=params(8),
         name="merge",
-    )(right_a, left_b, via_a, via_b)
+    )(right_a, left_b, from_left, from_right)
 
 
 def place_kernel(route_ref, *refs):
@@ -130,8 +135,12 @@
             slot = route_ref[side * half + i]
             mixed = []
             for c in range(CHUNKS):
-                own, left, right = (ref[i].astype(F32) for ref in refs[6 * c + side:6 * c + 6:2])
-                mixed.append(own + left + right)
+                own_a, own_b, first_left, first_right, left_a, right_b = refs[6 * c:6 * c + 6]
+                if side == 0:
+                    own, left, right = own_a[i], left_a[i], first_right[1, i]
+                else:
+                    own, left, right = own_b[i], first_left[1, i], right_b[i]
+                mixed.append(own.astype(F32) + left.astype(F32) + right.astype(F32))
             mean = sum(jnp.sum(m, axis=-1, keepdims=True) for m in mixed) / width
             centred = [m - mean for m in mixed]
             variance = sum(jnp.sum(m * m, axis=-1, keepdims=True) for m in centred) / width
@@ -216,29 +225,30 @@
     route = route[:, 0]
     rank = lax.axis_index("rank").astype(jnp.int32).reshape(1)
 
-    queries = project(features, w_qu, 0, width)
-    arrived = exchange(queries.reshape(slots, cands, width))
-    gate = project(after(features, queries), w_qu, width, width)
-    own = pick(route, arrived, users)
-    gathered = []
+    part = width // CHUNKS
+    near, own, queries = [], [], []
     for c in range(CHUNKS):
-        own_a, own_b = own[c]
-        if c > 0:
-            own_a, own_b = lax.optimization_barrier((own_a, own_b, *gathered[c - 1][2:6:3]))[:2]
-        left_a, left_b = rotate(own_a, 1), rotate(own_b, 1)
-        right_a, right_b = rotate(own_a, -1), rotate(own_b, -1)
-        far_a, far_b = rotate(left_a, 1), rotate(right_b, -1)
-        gathered.append([*own[c], left_a, left_b, right_a, right_b, far_a, far_b])
+        columns = w_qu[:, c * part:(c + 1) * part]
+        projected = jax.nn.silu(jnp.dot(features, columns, preferred_element_type=F32)).astype(BF16)
+        queries.append(projected.reshape(slots, cands, part))
+    gate = project(after(features, *queries), w_qu, width, width)
+    for c in range(CHUNKS):
+        arrived = exchange(queries[c])
+        own_a, own_b = pick(route, arrived, users)
+        own.append((own_a, own_b))
+        near.append([rotate(own_a, 1), rotate(own_b, 1), rotate(own_a, -1), rotate(own_b, -1)])
     parts = []
     for c in range(CHUNKS):
-        p_own_a, p_own_b, p_left_a, p_left_b, p_right_a, p_right_b, p_far_a, p_far_b = attend(
-            lengths, rank, gathered[c], hist_keys, hist_values, c
+        left_a, left_b, right_a, right_b = near[c]
+        if c > 0:
+            left_a, right_b = lax.optimization_barrier((left_a, right_b, parts[0]))[:2]
+        far_a, far_b = rotate(left_a, 1), rotate(right_b, -1)
+        p_own_a, p_own_b, go_right, go_left, p_right_a, p_left_b = attend(
+            lengths, rank, [*own[c], *near[c], far_a, far_b], hist_keys, hist_values, c
         )
-        via_a, via_b = rotate(p_far_a, 1), rotate(p_far_b, -1)
-        from_left_b, from_right_a = rotate(p_right_b, 1), rotate(p_left_a, -1)
-        to_right_a, to_left_b = merge(p_right_a, p_left_b, via_a, via_b)
-        from_left_a, from_right_b = rotate(to_right_a, 1), rotate(to_left_b, -1)
-        parts += [p_own_a, p_own_b, from_left_a, from_left_b, from_right_a, from_right_b]
+        from_left, from_right = rotate(go_right, 1), rotate(go_left, -1)
+        to_right, to_left = merge(p_right_a, p_left_b, from_left, from_right)
+        parts += [p_own_a, p_own_b, from_left, from_right, rotate(to_right, 1), rotate(to_left, -1)]
     normed = exchange(place(route, parts, slots)).reshape(slots * cands, width)
     ranked = finish(normed, gate, features, w_out)
     return ranked.reshape(1, slots, cands, width)

time: 165 us -> 155 us (0.939)
  blocking collectives: 37 us -> 0 us
  starting transfers between devices: 29.7 us -> 42.5 us
  waiting for transfers between devices: 62.1 us -> 71.9 us
  matrix products: 0 us -> 8.74 us
  Pallas kernels: 36 us -> 30.5 us
    all_to_all x1 -> x0, blocking collectives: 37 us -> none  [exchange(): return lax.all_to_all(x, 'cache', split_axis=0, concat_axis=0, tiled=True)]
    all_to_all x1 -> x3, waiting for transfers between devices: 23.8 us -> 42.2 us  [exchange(): return lax.all_to_all(x, 'cache', split_axis=0, concat_axis=0, tiled=True)]
    all_to_all x1 -> x3, starting transfers between devices: 4.81 us -> 19.5 us  [exchange(): return lax.all_to_all(x, 'cache', split_axis=0, concat_axis=0, tiled=True)]
    dot_general x0 -> x2, matrix products: none -> 8.74 us  [per_device(): jnp.dot(features, columns, preferred_element_type=F32)]
    ppermute x24 -> x20, waiting for transfers between devices: 38.2 us -> 29.7 us  [rotate(): return lax.ppermute(x, 'rank', [(i, (i + by) % n) for i in range(n)])]
    pallas_call x2 -> x1, Pallas kernels: 12.2 us -> 6.12 us  [project(): pl.pallas_call(project_kernel, grid=(steps,), in_specs=[pl.BlockSpec((blo...]
    ppermute x24 -> x20, starting transfers between devices: 24.8 us -> 23.1 us  [rotate(): return lax.ppermute(x, 'rank', [(i, (i + by) % n) for i in range(n)])]
  transfers between devices with their start and end apart: 25 -> 23, of which waited for: 17 -> 15; matrix products, arithmetic and copies ran while one was open for 0% -> 3% of each run, Pallas kernels for 12% -> 13%
where the time goes in v3:
time: 155 us; the launch traced here: 154 us
  waiting for transfers between devices  71.9 us (46%)
  starting transfers between devices  42.5 us (27%)
  Pallas kernels  30.5 us (20%)
  matrix products  8.74 us (6%)
    all_to_all x3, waiting for transfers between devices, exchange(): return lax.all_to_all(x, 'cache', split_axis=0, concat_axis=0, tiled=True)  42.2 us
    ppermute x20, waiting for transfers between devices, rotate(): return lax.ppermute(x, 'rank', [(i, (i + by) % n) for i in range(n)])  29.7 us
    ppermute x20, starting transfers between devices, rotate(): return lax.ppermute(x, 'rank', [(i, (i + by) % n) for i in range(n)])  23.1 us
    all_to_all x3, starting transfers between devices, exchange(): return lax.all_to_all(x, 'cache', split_axis=0, concat_axis=0, tiled=True)  19.5 us
    pallas_call x2, Pallas kernels, attend(): pl.pallas_call(attend_kernel, grid_spec=pltpu.PrefetchScalarGridSpec(num_...  13 us
    dot_general x2, matrix products, per_device(): jnp.dot(features, columns, preferred_element_type=F32)  8.74 us
    pallas_call x1, Pallas kernels, finish(): pl.pallas_call(finish_kernel, grid=(steps,), in_specs=[rows_spec] * 3 + [...  7.04 us
    pallas_call x1, Pallas kernels, project(): pl.pallas_call(project_kernel, grid=(steps,), in_specs=[pl.BlockSpec((blo...  6.12 us
  transfers between devices with their start and end apart: 23, of which 15 were waited for; matrix products, arithmetic and copies ran while one was open for 3% of the time, Pallas kernels for 13%

profile of v3, /device:TPU:6, one launch (start us, length us, event | category | flops | bytes accessed | tf_op | source)
XLA Modules:
  0.0 153.9 jit_solution(17936563334466629107)
XLA Ops:
  0.0 4.4 %multiply_convert_fusion.1 = bf16[1024,512]{1,0:T(8,128)(2,1)} fusion(bf16[1024,1024]{1,0:T(8,128)(2,1)} %bitcast.18, bf16[1024,2048]{1,0:T(8,128)(2,1)} %w_ref.2), kind=kOutput, calls=%fused_computation.1 | convolution fusion | flops 1076363264 | bytes 4194304 | tf_op jit(solution)/shard_map/dot_general | solution.py:232
  4.4 8.3 %all-to-all-start = ((bf16[32,32,512]{2,1,0:T(8,128)(2,1)}), bf16[32,32,512]{2,1,0:T(8,128)(2,1)S(1)}, u32[]{:S(2)}, u32[]{:S(2)}) async-start(bf16[32,32,512]{2,1,0:T(8,128)(2,1)} %bitcast.3), calls=%async_computation | async-start | bytes 2097152 | tf_op jit(solution)/shard_map/all_to_all | solution.py:214
  12.7 4.4 %multiply_convert_fusion = bf16[1024,512]{1,0:T(8,128)(2,1)} fusion(bf16[1024,1024]{1,0:T(8,128)(2,1)} %bitcast.19, bf16[1024,2048]{1,0:T(8,128)(2,1)} %w_ref.2), kind=kOutput, calls=%fused_computation | convolution fusion | flops 1076363264 | bytes 4194304 | tf_op jit(solution)/shard_map/dot_general | solution.py:232
  17.1 13.0 %all-to-all-done.arrived_ref = bf16[32,32,512]{2,1,0:T(8,128)(2,1)S(1)} async-done(((bf16[32,32,512]{2,1,0:T(8,128)(2,1)}), bf16[32,32,512]{2,1,0:T(8,128)(2,1)S(1)}, u32[]{:S(2)}, u32[]{:S(2)}) %all-to-all-start) | async-done | bytes 1048608 | tf_op jit(solution)/shard_map/all_to_all | solution.py:214
  30.0 4.1 %all-to-all-start.1 = ((bf16[32,32,512]{2,1,0:T(8,128)(2,1)}), bf16[32,32,512]{2,1,0:T(8,128)(2,1)S(1)}, u32[]{:S(2)}, u32[]{:S(2)}) async-start(bf16[32,32,512]{2,1,0:T(8,128)(2,1)} %bitcast.6), calls=%async_computation.1 | async-start | bytes 2097152 | tf_op jit(solution)/shard_map/all_to_all | solution.py:214
  35.3 1.5 %collective-permute-start.3 = (bf16[8,32,512]{2,1,0:T(8,128)(2,1)S(1)}, bf16[8,32,512]{2,1,0:T(8,128)(2,1)S(1)}, u32[]{:S(2)}, u32[]{:S(2)}) collective-permute-start(bf16[8,32,512]{2,1,0:T(8,128)(2,1)S(1)} %get-tuple-element.29.refs_1_), channel_id=1, source_target_pairs={{0,3},{1,0},{2,1},{3,2},{4,7},{5,4},{6,5},{7,6},{8,11},{9,8},{10,9... | collective-permute-start | bytes 786440 | tf_op jit(solution)/shard_map/ppermute | solution.py:210
  37.6 2.4 %collective-permute-start.1 = (bf16[8,32,512]{2,1,0:T(8,128)(2,1)S(1)}, bf16[8,32,512]{2,1,0:T(8,128)(2,1)S(1)}, u32[]{:S(2)}, u32[]{:S(2)}) collective-permute-start(bf16[8,32,512]{2,1,0:T(8,128)(2,1)S(1)} %get-tuple-element.29.refs_1_), channel_id=1, source_target_pairs={{0,1},{1,2},{2,3},{3,0},{4,5},{5,6},{6,7},{7,4},{8,9},{9,10},{10,1... | collective-permute-start | bytes 786440 | tf_op jit(solution)/shard_map/ppermute | solution.py:210
  40.0 3.9 %collective-permute-done.refs_2_ = bf16[8,32,512]{2,1,0:T(8,128)(2,1)S(1)} collective-permute-done((bf16[8,32,512]{2,1,0:T(8,128)(2,1)S(1)}, bf16[8,32,512]{2,1,0:T(8,128)(2,1)S(1)}, u32[]{:S(2)}, u32[]{:S(2)}) %collective-permute-start) | collective-permute-done | bytes 262176 | tf_op jit(solution)/shard_map/ppermute | solution.py:210
  43.9 1.7 %collective-permute-start.4 = (bf16[8,32,512]{2,1,0:T(8,128)(2,1)S(1)}, bf16[8,32,512]{2,1,0:T(8,128)(2,1)}, u32[]{:S(2)}, u32[]{:S(2)}) collective-permute-start(bf16[8,32,512]{2,1,0:T(8,128)(2,1)S(1)} %collective-permute-done.refs_2_), channel_id=1, source_target_pairs={{0,1},{1,2},{2,3},{3,0},{4,5},{5,6},{6,7},{7,4},{8,9},{9,10},{10,1... | collective-permute-start | bytes 786440 | tf_op jit(solution)/shard_map/ppermute | solution.py:210
  46.0 5.5 %all-to-all-done.1.arrived_ref = bf16[32,32,512]{2,1,0:T(8,128)(2,1)S(1)} async-done(((bf16[32,32,512]{2,1,0:T(8,128)(2,1)}), bf16[32,32,512]{2,1,0:T(8,128)(2,1)S(1)}, u32[]{:S(2)}, u32[]{:S(2)}) %all-to-all-start.1) | async-done | bytes 1048608 | tf_op jit(solution)/shard_map/all_to_all | solution.py:214
  52.6 1.5 %collective-permute-start.13 = (bf16[8,32,512]{2,1,0:T(8,128)(2,1)S(1)}, bf16[8,32,512]{2,1,0:T(8,128)(2,1)S(1)}, u32[]{:S(2)}, u32[]{:S(2)}) collective-permute-start(bf16[8,32,512]{2,1,0:T(8,128)(2,1)S(1)} %get-tuple-element.39.refs_1_), channel_id=1, source_target_pairs={{0,3},{1,0},{2,1},{3,2},{4,7},{5,4},{6,5},{7,6},{8,11},{9,8},{10,9... | collective-permute-start | bytes 786440 | tf_op jit(solution)/shard_map/ppermute | solution.py:210
  55.0 2.4 %collective-permute-start.11 = (bf16[8,32,512]{2,1,0:T(8,128)(2,1)S(1)}, bf16[8,32,512]{2,1,0:T(8,128)(2,1)S(1)}, u32[]{:S(2)}, u32[]{:S(2)}) collective-permute-start(bf16[8,32,512]{2,1,0:T(8,128)(2,1)S(1)} %get-tuple-element.39.refs_1_), channel_id=1, source_target_pairs={{0,1},{1,2},{2,3},{3,0},{4,5},{5,6},{6,7},{7,4},{8,9},{9,10},{10,1... | collective-permute-start | bytes 786440 | tf_op jit(solution)/shard_map/ppermute | solution.py:210
  57.4 6.6 %attend.2 = (bf16[8,32,512]{2,1,0:T(8,128)(2,1)S(1)}, bf16[8,32,512]{2,1,0:T(8,128)(2,1)S(1)}, bf16[2,8,32,512]{3,2,1,0:T(8,128)(2,1)S(1)}, bf16[2,8,32,512]{3,2...) custom-call(s32[16]{0:T(128)S(1)} %copy-done.1, s32[1]{0:T(128)} %bitcast.1.rank_ref, ...), custom_call_target="tpu_custom_call" | custom-call | tf_op jit(solution)/shard_map/attend/pallas_call | solution.py:98
  64.5 1.5 %collective-permute-start.15 = (bf16[8,32,512]{2,1,0:T(8,128)(2,1)S(1)}, bf16[8,32,512]{2,1,0:T(8,128)(2,1)S(1)}, u32[]{:S(2)}, u32[]{:S(2)}) collective-permute-start(bf16[8,32,512]{2,1,0:T(8,128)(2,1)S(1)} %collective-permute-done.13.refs_5_), channel_id=1, source_target_pairs={{0,3},{1,0},{2,1},{3,2},{4,7},{5,4},{6,5},{7,6},{8,11},{9,8},{10,9... | collective-permute-start | bytes 786440 | tf_op jit(solution)/shard_map/ppermute | solution.py:210
  66.1 1.7 %collective-permute-start.6 = (bf16[2,8,32,512]{3,2,1,0:T(8,128)(2,1)S(1)}, bf16[2,8,32,512]{3,2,1,0:T(8,128)(2,1)S(1)}, u32[]{:S(2)}, u32[]{:S(2)}) collective-permute-start(bf16[2,8,32,512]{3,2,1,0:T(8,128)(2,1)S(1)} %get-tuple-element.32), channel_id=1, source_target_pairs={{0,1},{1,2},{2,3},{3,0},{4,5},{5,6},{6,7},{7,4},{8,9},{9,10},{10,1... | collective-permute-start | bytes 1572872 | tf_op jit(solution)/shard_map/ppermute | solution.py:210
  68.2 5.1 %collective-permute-done.14.refs_6_ = bf16[8,32,512]{2,1,0:T(8,128)(2,1)S(1)} collective-permute-done((bf16[8,32,512]{2,1,0:T(8,128)(2,1)S(1)}, bf16[8,32,512]{2,1,0:T(8,128)(2,1)S(1)}, u32[]{:S(2)}, u32[]{:S(2)}) %collective-permute-start.14) | collective-permute-done | bytes 262176 | tf_op jit(solution)/shard_map/ppermute | solution.py:210
  73.3 1.7 %collective-permute-done.15.refs_7_ = bf16[8,32,512]{2,1,0:T(8,128)(2,1)S(1)} collective-permute-done((bf16[8,32,512]{2,1,0:T(8,128)(2,1)S(1)}, bf16[8,32,512]{2,1,0:T(8,128)(2,1)S(1)}, u32[]{:S(2)}, u32[]{:S(2)}) %collective-permute-start.15) | collective-permute-done | bytes 262176 | tf_op jit(solution)/shard_map/ppermute | solution.py:210
  75.0 6.4 %attend.3 = (bf16[8,32,512]{2,1,0:T(8,128)(2,1)S(1)}, bf16[8,32,512]{2,1,0:T(8,128)(2,1)S(1)}, bf16[2,8,32,512]{3,2,1,0:T(8,128)(2,1)S(1)}, bf16[2,8,32,512]{3,2...) custom-call(s32[16]{0:T(128)S(1)} %copy-done.1, s32[1]{0:T(128)} %bitcast.1.rank_ref, ...), custom_call_target="tpu_custom_call" | custom-call | tf_op jit(solution)/shard_map/attend/pallas_call | solution.py:98
  81.5 2.0 %collective-permute-start.17 = (bf16[2,8,32,512]{3,2,1,0:T(8,128)(2,1)S(1)}, bf16[2,8,32,512]{3,2,1,0:T(8,128)(2,1)S(1)}, u32[]{:S(2)}, u32[]{:S(2)}) collective-permute-start(bf16[2,8,32,512]{3,2,1,0:T(8,128)(2,1)S(1)} %get-tuple-element.45), channel_id=1, source_target_pairs={{0,3},{1,0},{2,1},{3,2},{4,7},{5,4},{6,5},{7,6},{8,11},{9,8},{10,9... | collective-permute-start | bytes 1572872 | tf_op jit(solution)/shard_map/ppermute | solution.py:210
  84.5 1.7 %collective-permute-done.7.from_right_ref.refs_3_ = bf16[2,8,32,512]{3,2,1,0:T(8,128)(2,1)S(1)} collective-permute-done((bf16[2,8,32,512]{3,2,1,0:T(8,128)(2,1)S(1)}, bf16[2,8,32,512]{3,2,1,0:T(8,128)(2,1)S(1)}, u32[]{:S(2)}, u32[]{:S(2)}) %collective-permute-start.7) | collective-permute-done | bytes 524320 | tf_op jit(solution)/shard_map/ppermute | solution.py:210
  86.4 2.0 %collective-permute-start.9 = (bf16[8,32,512]{2,1,0:T(8,128)(2,1)S(1)}, bf16[8,32,512]{2,1,0:T(8,128)(2,1)S(1)}, u32[]{:S(2)}, u32[]{:S(2)}) collective-permute-start(bf16[8,32,512]{2,1,0:T(8,128)(2,1)S(1)} %get-tuple-element.37), channel_id=1, source_target_pairs={{0,3},{1,0},{2,1},{3,2},{4,7},{5,4},{6,5},{7,6},{8,11},{9,8},{10,9... | collective-permute-start | bytes 786440 | tf_op jit(solution)/shard_map/ppermute | solution.py:210
  88.4 7.9 %collective-permute-done.16.from_left_ref.refs_8_ = bf16[2,8,32,512]{3,2,1,0:T(8,128)(2,1)S(1)} collective-permute-done((bf16[2,8,32,512]{3,2,1,0:T(8,128)(2,1)S(1)}, bf16[2,8,32,512]{3,2,1,0:T(8,128)(2,1)S(1)}, u32[]{:S(2)}, u32[]{:S(2)}) %collective-permute-start.16) | collective-permute-done | bytes 524320 | tf_op jit(solution)/shard_map/ppermute | solution.py:210
  97.8 2.0 %collective-permute-start.19 = (bf16[8,32,512]{2,1,0:T(8,128)(2,1)S(1)}, bf16[8,32,512]{2,1,0:T(8,128)(2,1)S(1)}, u32[]{:S(2)}, u32[]{:S(2)}) collective-permute-start(bf16[8,32,512]{2,1,0:T(8,128)(2,1)S(1)} %get-tuple-element.49), channel_id=1, source_target_pairs={{0,3},{1,0},{2,1},{3,2},{4,7},{5,4},{6,5},{7,6},{8,11},{9,8},{10,9... | collective-permute-start | bytes 786440 | tf_op jit(solution)/shard_map/ppermute | solution.py:210
  99.8 2.1 %collective-permute-done.8.refs_4_ = bf16[8,32,512]{2,1,0:T(8,128)(2,1)S(1)} collective-permute-done((bf16[8,32,512]{2,1,0:T(8,128)(2,1)S(1)}, bf16[8,32,512]{2,1,0:T(8,128)(2,1)S(1)}, u32[]{:S(2)}, u32[]{:S(2)}) %collective-permute-start.8) | collective-permute-done | bytes 262176 | tf_op jit(solution)/shard_map/ppermute | solution.py:210
  101.9 1.3 collective-permute-done.9.refs_5_
  103.2 2.2 %collective-permute-done.18.refs_10_ = bf16[8,32,512]{2,1,0:T(8,128)(2,1)S(1)} collective-permute-done((bf16[8,32,512]{2,1,0:T(8,128)(2,1)S(1)}, bf16[8,32,512]{2,1,0:T(8,128)(2,1)S(1)}, u32[]{:S(2)}, u32[]{:S(2)}) %collective-permute-start.18) | collective-permute-done | bytes 262176 | tf_op jit(solution)/shard_map/ppermute | solution.py:210
  105.4 1.4 collective-permute-done.19.refs_11_
  106.8 3.0 %place.1 = bf16[32,32,1024]{2,1,0:T(8,128)(2,1)} custom-call(s32[16]{0:T(128)S(1)} %bitcast.13, bf16[8,32,512]{2,1,0:T(8,128)(2,1)S(1)} %get-tuple-element.30.refs_0_, bf16[8,32,512]{2,1,0:T(8,128)(2,1)S(1)} %get-tuple-element.31.refs_1_, bf16[2,8,32,512]{3,2,1,0:T(8,128)(2,1)S(1)} %collective-permute-done.6.from_left_ref.refs_2_, ...), custom_call_target="tpu_custom_call" | custom-call | tf_op jit(solution)/shard_map/place/pallas_call | solution.py:154
  109.8 7.1 %all-to-all-start.2 = ((bf16[32,32,1024]{2,1,0:T(8,128)(2,1)}), bf16[32,32,1024]{2,1,0:T(8,128)(2,1)}, u32[]{:S(2)}, u32[]{:S(2)}) async-start(bf16[32,32,1024]{2,1,0:T(8,128)(2,1)} %place.1), calls=%async_computation.2 | async-start | bytes 4194304 | tf_op jit(solution)/shard_map/all_to_all | solution.py:214
  116.9 6.1 %project.1.gate_ref = bf16[1024,1024]{1,0:T(8,128)(2,1)} custom-call(bf16[1024,1024]{1,0:T(8,128)(2,1)} %bitcast.20, bf16[1024,2048]{1,0:T(8,128)(2,1)} %w_ref.2), custom_call_target="tpu_custom_call" | custom-call | tf_op jit(solution)/shard_map/project/pallas_call | solution.py:174
  123.0 23.8 %all-to-all-done.2 = bf16[32,32,1024]{2,1,0:T(8,128)(2,1)} async-done(((bf16[32,32,1024]{2,1,0:T(8,128)(2,1)}), bf16[32,32,1024]{2,1,0:T(8,128)(2,1)}, u32[]{:S(2)}, u32[]{:S(2)}) %all-to-all-start.2) | async-done | bytes 2097184 | tf_op jit(solution)/shard_map/all_to_all | solution.py:214
  146.9 7.0 %finish.1 = bf16[1024,1024]{1,0:T(8,128)(2,1)} custom-call(bf16[1024,1024]{1,0:T(8,128)(2,1)} %bitcast.7.normed_ref, bf16[1024,1024]{1,0:T(8,128)(2,1)} %project.1.gate_ref, bf16[1024,1024]{1,0:T(8,128)(2,1)} %bitcast.21, bf16[1024,1024]{1,0:T(8,128)(2,1)} %w_ref.3), custom_call_target="tpu_custom_call" | custom-call | tf_op jit(solution)/shard_map/finish/pallas_call | solution.py:197
  (29 shorter events, 8.1 us)
Async XLA Ops:
  4.4 25.7 %all-to-all-start = ((bf16[32,32,512]{2,1,0:T(8,128)(2,1)}), bf16[32,32,512]{2,1,0:T(8,128)(2,1)S(1)}, u32[]{:S(2)}, u32[]{:S(2)}) async-start(bf16[32,32,512]{2,1,0:T(8,128)(2,1)} %bitcast.3), calls=%async_computation | async-start | bytes 2097152 | tf_op jit(solution)/shard_map/all_to_all | solution.py:214
  17.1 17.0 %copy-start = (s32[16,1]{0,1:T(1,128)S(1)}, s32[16,1]{0,1:T(1,128)}, u32[]{:S(2)}) copy-start(s32[16,1]{0,1:T(1,128)} %param.10) | copy-start | bytes 196
  30.0 27.3 %copy-start.1 = (s32[16]{0:T(128)S(1)}, s32[16]{0:T(128)}, u32[]{:S(2)}) copy-start(s32[16]{0:T(128)} %lengths_ref.3) | copy-start | bytes 196
  30.0 21.4 %all-to-all-start.1 = ((bf16[32,32,512]{2,1,0:T(8,128)(2,1)}), bf16[32,32,512]{2,1,0:T(8,128)(2,1)S(1)}, u32[]{:S(2)}, u32[]{:S(2)}) async-start(bf16[32,32,512]{2,1,0:T(8,128)(2,1)} %bitcast.6), calls=%async_computation.1 | async-start | bytes 2097152 | tf_op jit(solution)/shard_map/all_to_all | solution.py:214
  34.7 9.2 %collective-permute-start = (bf16[8,32,512]{2,1,0:T(8,128)(2,1)S(1)}, bf16[8,32,512]{2,1,0:T(8,128)(2,1)S(1)}, u32[]{:S(2)}, u32[]{:S(2)}) collective-permute-start(bf16[8,32,512]{2,1,0:T(8,128)(2,1)S(1)} %get-tuple-element.28.refs_0_), channel_id=1, source_target_pairs={{0,1},{1,2},{2,3},{3,0},{4,5},{5,6},{6,7},{7,4},{8,9},{9,10},{10,1... | collective-permute-start | bytes 786440 | tf_op jit(solution)/shard_map/ppermute | solution.py:210
  35.3 10.4 %collective-permute-start.3 = (bf16[8,32,512]{2,1,0:T(8,128)(2,1)S(1)}, bf16[8,32,512]{2,1,0:T(8,128)(2,1)S(1)}, u32[]{:S(2)}, u32[]{:S(2)}) collective-permute-start(bf16[8,32,512]{2,1,0:T(8,128)(2,1)S(1)} %get-tuple-element.29.refs_1_), channel_id=1, source_target_pairs={{0,3},{1,0},{2,1},{3,2},{4,7},{5,4},{6,5},{7,6},{8,11},{9,8},{10,9... | collective-permute-start | bytes 786440 | tf_op jit(solution)/shard_map/ppermute | solution.py:210
  36.8 15.8 %collective-permute-start.2 = (bf16[8,32,512]{2,1,0:T(8,128)(2,1)S(1)}, bf16[8,32,512]{2,1,0:T(8,128)(2,1)S(1)}, u32[]{:S(2)}, u32[]{:S(2)}) collective-permute-start(bf16[8,32,512]{2,1,0:T(8,128)(2,1)S(1)} %get-tuple-element.28.refs_0_), channel_id=1, source_target_pairs={{0,3},{1,0},{2,1},{3,2},{4,7},{5,4},{6,5},{7,6},{8,11},{9,8},{10,9... | collective-permute-start | bytes 786440 | tf_op jit(solution)/shard_map/ppermute | solution.py:210
  37.6 16.5 %collective-permute-start.1 = (bf16[8,32,512]{2,1,0:T(8,128)(2,1)S(1)}, bf16[8,32,512]{2,1,0:T(8,128)(2,1)S(1)}, u32[]{:S(2)}, u32[]{:S(2)}) collective-permute-start(bf16[8,32,512]{2,1,0:T(8,128)(2,1)S(1)} %get-tuple-element.29.refs_1_), channel_id=1, source_target_pairs={{0,1},{1,2},{2,3},{3,0},{4,5},{5,6},{6,7},{7,4},{8,9},{9,10},{10,1... | collective-permute-start | bytes 786440 | tf_op jit(solution)/shard_map/ppermute | solution.py:210
  43.9 11.1 %collective-permute-start.4 = (bf16[8,32,512]{2,1,0:T(8,128)(2,1)S(1)}, bf16[8,32,512]{2,1,0:T(8,128)(2,1)}, u32[]{:S(2)}, u32[]{:S(2)}) collective-permute-start(bf16[8,32,512]{2,1,0:T(8,128)(2,1)S(1)} %collective-permute-done.refs_2_), channel_id=1, source_target_pairs={{0,1},{1,2},{2,3},{3,0},{4,5},{5,6},{6,7},{7,4},{8,9},{9,10},{10,1... | collective-permute-start | bytes 786440 | tf_op jit(solution)/shard_map/ppermute | solution.py:210
  45.7 11.7 %collective-permute-start.5 = (bf16[8,32,512]{2,1,0:T(8,128)(2,1)S(1)}, bf16[8,32,512]{2,1,0:T(8,128)(2,1)}, u32[]{:S(2)}, u32[]{:S(2)}) collective-permute-start(bf16[8,32,512]{2,1,0:T(8,128)(2,1)S(1)} %collective-permute-done.3.refs_5_), channel_id=1, source_target_pairs={{0,3},{1,0},{2,1},{3,2},{4,7},{5,4},{6,5},{7,6},{8,11},{9,8},{10,9... | collective-permute-start | bytes 786440 | tf_op jit(solution)/shard_map/ppermute | solution.py:210
  52.0 11.9 %collective-permute-start.10 = (bf16[8,32,512]{2,1,0:T(8,128)(2,1)S(1)}, bf16[8,32,512]{2,1,0:T(8,128)(2,1)S(1)}, u32[]{:S(2)}, u32[]{:S(2)}) collective-permute-start(bf16[8,32,512]{2,1,0:T(8,128)(2,1)S(1)} %get-tuple-element.38.refs_0_), channel_id=1, source_target_pairs={{0,1},{1,2},{2,3},{3,0},{4,5},{5,6},{6,7},{7,4},{8,9},{9,10},{10,1... | collective-permute-start | bytes 786440 | tf_op jit(solution)/shard_map/ppermute | solution.py:210
  52.6 11.4 %collective-permute-start.13 = (bf16[8,32,512]{2,1,0:T(8,128)(2,1)S(1)}, bf16[8,32,512]{2,1,0:T(8,128)(2,1)S(1)}, u32[]{:S(2)}, u32[]{:S(2)}) collective-permute-start(bf16[8,32,512]{2,1,0:T(8,128)(2,1)S(1)} %get-tuple-element.39.refs_1_), channel_id=1, source_target_pairs={{0,3},{1,0},{2,1},{3,2},{4,7},{5,4},{6,5},{7,6},{8,11},{9,8},{10,9... | collective-permute-start | bytes 786440 | tf_op jit(solution)/shard_map/ppermute | solution.py:210
  54.1 13.7 %collective-permute-start.12 = (bf16[8,32,512]{2,1,0:T(8,128)(2,1)S(1)}, bf16[8,32,512]{2,1,0:T(8,128)(2,1)S(1)}, u32[]{:S(2)}, u32[]{:S(2)}) collective-permute-start(bf16[8,32,512]{2,1,0:T(8,128)(2,1)S(1)} %get-tuple-element.38.refs_0_), channel_id=1, source_target_pairs={{0,3},{1,0},{2,1},{3,2},{4,7},{5,4},{6,5},{7,6},{8,11},{9,8},{10,9... | collective-permute-start | bytes 786440 | tf_op jit(solution)/shard_map/ppermute | solution.py:210
  55.0 13.2 %collective-permute-start.11 = (bf16[8,32,512]{2,1,0:T(8,128)(2,1)S(1)}, bf16[8,32,512]{2,1,0:T(8,128)(2,1)S(1)}, u32[]{:S(2)}, u32[]{:S(2)}) collective-permute-start(bf16[8,32,512]{2,1,0:T(8,128)(2,1)S(1)} %get-tuple-element.39.refs_1_), channel_id=1, source_target_pairs={{0,1},{1,2},{2,3},{3,0},{4,5},{5,6},{6,7},{7,4},{8,9},{9,10},{10,1... | collective-permute-start | bytes 786440 | tf_op jit(solution)/shard_map/ppermute | solution.py:210
  64.0 9.3 %collective-permute-start.14 = (bf16[8,32,512]{2,1,0:T(8,128)(2,1)S(1)}, bf16[8,32,512]{2,1,0:T(8,128)(2,1)S(1)}, u32[]{:S(2)}, u32[]{:S(2)}) collective-permute-start(bf16[8,32,512]{2,1,0:T(8,128)(2,1)S(1)} %collective-permute-done.10.refs_2_), channel_id=1, source_target_pairs={{0,1},{1,2},{2,3},{3,0},{4,5},{5,6},{6,7},{7,4},{8,9},{9,10},{10,1... | collective-permute-start | bytes 786440 | tf_op jit(solution)/shard_map/ppermute | solution.py:210
  64.5 10.5 %collective-permute-start.15 = (bf16[8,32,512]{2,1,0:T(8,128)(2,1)S(1)}, bf16[8,32,512]{2,1,0:T(8,128)(2,1)S(1)}, u32[]{:S(2)}, u32[]{:S(2)}) collective-permute-start(bf16[8,32,512]{2,1,0:T(8,128)(2,1)S(1)} %collective-permute-done.13.refs_5_), channel_id=1, source_target_pairs={{0,3},{1,0},{2,1},{3,2},{4,7},{5,4},{6,5},{7,6},{8,11},{9,8},{10,9... | collective-permute-start | bytes 786440 | tf_op jit(solution)/shard_map/ppermute | solution.py:210
  66.1 18.5 %collective-permute-start.6 = (bf16[2,8,32,512]{3,2,1,0:T(8,128)(2,1)S(1)}, bf16[2,8,32,512]{3,2,1,0:T(8,128)(2,1)S(1)}, u32[]{:S(2)}, u32[]{:S(2)}) collective-permute-start(bf16[2,8,32,512]{3,2,1,0:T(8,128)(2,1)S(1)} %get-tuple-element.32), channel_id=1, source_target_pairs={{0,1},{1,2},{2,3},{3,0},{4,5},{5,6},{6,7},{7,4},{8,9},{9,10},{10,1... | collective-permute-start | bytes 1572872 | tf_op jit(solution)/shard_map/ppermute | solution.py:210
  67.8 18.4 %collective-permute-start.7 = (bf16[2,8,32,512]{3,2,1,0:T(8,128)(2,1)S(1)}, bf16[2,8,32,512]{3,2,1,0:T(8,128)(2,1)S(1)}, u32[]{:S(2)}, u32[]{:S(2)}) collective-permute-start(bf16[2,8,32,512]{3,2,1,0:T(8,128)(2,1)S(1)} %get-tuple-element.33), channel_id=1, source_target_pairs={{0,3},{1,0},{2,1},{3,2},{4,7},{5,4},{6,5},{7,6},{8,11},{9,8},{10,9... | collective-permute-start | bytes 1572872 | tf_op jit(solution)/shard_map/ppermute | solution.py:210
  81.4 14.9 %collective-permute-start.16 = (bf16[2,8,32,512]{3,2,1,0:T(8,128)(2,1)S(1)}, bf16[2,8,32,512]{3,2,1,0:T(8,128)(2,1)S(1)}, u32[]{:S(2)}, u32[]{:S(2)}) collective-permute-start(bf16[2,8,32,512]{3,2,1,0:T(8,128)(2,1)S(1)} %get-tuple-element.44), channel_id=1, source_target_pairs={{0,1},{1,2},{2,3},{3,0},{4,5},{5,6},{6,7},{7,4},{8,9},{9,10},{10,1... | collective-permute-start | bytes 1572872 | tf_op jit(solution)/shard_map/ppermute | solution.py:210
  81.5 16.1 %collective-permute-start.17 = (bf16[2,8,32,512]{3,2,1,0:T(8,128)(2,1)S(1)}, bf16[2,8,32,512]{3,2,1,0:T(8,128)(2,1)S(1)}, u32[]{:S(2)}, u32[]{:S(2)}) collective-permute-start(bf16[2,8,32,512]{3,2,1,0:T(8,128)(2,1)S(1)} %get-tuple-element.45), channel_id=1, source_target_pairs={{0,3},{1,0},{2,1},{3,2},{4,7},{5,4},{6,5},{7,6},{8,11},{9,8},{10,9... | collective-permute-start | bytes 1572872 | tf_op jit(solution)/shard_map/ppermute | solution.py:210
  86.3 15.6 %collective-permute-start.8 = (bf16[8,32,512]{2,1,0:T(8,128)(2,1)S(1)}, bf16[8,32,512]{2,1,0:T(8,128)(2,1)S(1)}, u32[]{:S(2)}, u32[]{:S(2)}) collective-permute-start(bf16[8,32,512]{2,1,0:T(8,128)(2,1)S(1)} %get-tuple-element.36), channel_id=1, source_target_pairs={{0,1},{1,2},{2,3},{3,0},{4,5},{5,6},{6,7},{7,4},{8,9},{9,10},{10,1... | collective-permute-start | bytes 786440 | tf_op jit(solution)/shard_map/ppermute | solution.py:210
  86.4 16.8 %collective-permute-start.9 = (bf16[8,32,512]{2,1,0:T(8,128)(2,1)S(1)}, bf16[8,32,512]{2,1,0:T(8,128)(2,1)S(1)}, u32[]{:S(2)}, u32[]{:S(2)}) collective-permute-start(bf16[8,32,512]{2,1,0:T(8,128)(2,1)S(1)} %get-tuple-element.37), channel_id=1, source_target_pairs={{0,3},{1,0},{2,1},{3,2},{4,7},{5,4},{6,5},{7,6},{8,11},{9,8},{10,9... | collective-permute-start | bytes 786440 | tf_op jit(solution)/shard_map/ppermute | solution.py:210
  97.7 7.6 %collective-permute-start.18 = (bf16[8,32,512]{2,1,0:T(8,128)(2,1)S(1)}, bf16[8,32,512]{2,1,0:T(8,128)(2,1)S(1)}, u32[]{:S(2)}, u32[]{:S(2)}) collective-permute-start(bf16[8,32,512]{2,1,0:T(8,128)(2,1)S(1)} %get-tuple-element.48), channel_id=1, source_target_pairs={{0,1},{1,2},{2,3},{3,0},{4,5},{5,6},{6,7},{7,4},{8,9},{9,10},{10,1... | collective-permute-start | bytes 786440 | tf_op jit(solution)/shard_map/ppermute | solution.py:210
  97.8 9.0 %collective-permute-start.19 = (bf16[8,32,512]{2,1,0:T(8,128)(2,1)S(1)}, bf16[8,32,512]{2,1,0:T(8,128)(2,1)S(1)}, u32[]{:S(2)}, u32[]{:S(2)}) collective-permute-start(bf16[8,32,512]{2,1,0:T(8,128)(2,1)S(1)} %get-tuple-element.49), channel_id=1, source_target_pairs={{0,3},{1,0},{2,1},{3,2},{4,7},{5,4},{6,5},{7,6},{8,11},{9,8},{10,9... | collective-permute-start | bytes 786440 | tf_op jit(solution)/shard_map/ppermute | solution.py:210
  109.8 37.0 %all-to-all-start.2 = ((bf16[32,32,1024]{2,1,0:T(8,128)(2,1)}), bf16[32,32,1024]{2,1,0:T(8,128)(2,1)}, u32[]{:S(2)}, u32[]{:S(2)}) async-start(bf16[32,32,1024]{2,1,0:T(8,128)(2,1)} %place.1), calls=%async_computation.2 | async-start | bytes 4194304 | tf_op jit(solution)/shard_map/all_to_all | solution.py:214

commit v4 on v3

--- a/solution.py
+++ b/solution.py
@@ -83,7 +83,7 @@
             out[u, :, cols] = mixed[n * cands:(n + 1) * cands]
 
 
-def attend(lengths, rank, queries, keys, values, chunk, group=2):
+def attend(lengths, rank, queries, keys, values, chunk, group=4):
     half, cands, width = queries[0].shape
     events = keys.shape[1]
 

time: 155 us -> 154 us (level)
  no operation moved by 1% of the time
where the time goes in v4:
time: 154 us
  waiting for transfers between devices  73 us (47%)
  starting transfers between devices  42.6 us (28%)
  Pallas kernels  29.4 us (19%)
  matrix products  8.74 us (6%)
    all_to_all x3, waiting for transfers between devices, exchange(): return lax.all_to_all(x, 'cache', split_axis=0, concat_axis=0, tiled=True)  42.2 us
    ppermute x20, waiting for transfers between devices, rotate(): return lax.ppermute(x, 'rank', [(i, (i + by) % n) for i in range(n)])  30.8 us
    ppermute x20, starting transfers between devices, rotate(): return lax.ppermute(x, 'rank', [(i, (i + by) % n) for i in range(n)])  23.1 us
    all_to_all x3, starting transfers between devices, exchange(): return lax.all_to_all(x, 'cache', split_axis=0, concat_axis=0, tiled=True)  19.5 us
    pallas_call x2, Pallas kernels, attend(): pl.pallas_call(attend_kernel, grid_spec=pltpu.PrefetchScalarGridSpec(num_...  11.8 us
    dot_general x2, matrix products, per_device(): jnp.dot(features, columns, preferred_element_type=F32)  8.74 us
    pallas_call x1, Pallas kernels, finish(): pl.pallas_call(finish_kernel, grid=(steps,), in_specs=[rows_spec] * 3 + [...  7.04 us
    pallas_call x1, Pallas kernels, project(): pl.pallas_call(project_kernel, grid=(steps,), in_specs=[pl.BlockSpec((blo...  6.12 us
  transfers between devices with their start and end apart: 23, of which 15 were waited for; matrix products, arithmetic and copies ran while one was open for 3% of the time, Pallas kernels for 13%

profile of v4, /device:TPU:6, one launch (start us, length us, event | category | flops | bytes accessed | tf_op | source)
XLA Modules:
  0.0 153.9 jit_solution(18221838177586263079)
XLA Ops:
  0.0 4.4 %multiply_convert_fusion.1 = bf16[1024,512]{1,0:T(8,128)(2,1)} fusion(bf16[1024,1024]{1,0:T(8,128)(2,1)} %bitcast.18, bf16[1024,2048]{1,0:T(8,128)(2,1)} %w_ref.2), kind=kOutput, calls=%fused_computation.1 | convolution fusion | flops 1076363264 | bytes 4194304 | tf_op jit(solution)/shard_map/dot_general | solution.py:232
  4.4 8.3 %all-to-all-start = ((bf16[32,32,512]{2,1,0:T(8,128)(2,1)}), bf16[32,32,512]{2,1,0:T(8,128)(2,1)S(1)}, u32[]{:S(2)}, u32[]{:S(2)}) async-start(bf16[32,32,512]{2,1,0:T(8,128)(2,1)} %bitcast.3), calls=%async_computation | async-start | bytes 2097152 | tf_op jit(solution)/shard_map/all_to_all | solution.py:214
  12.7 4.4 %multiply_convert_fusion = bf16[1024,512]{1,0:T(8,128)(2,1)} fusion(bf16[1024,1024]{1,0:T(8,128)(2,1)} %bitcast.19, bf16[1024,2048]{1,0:T(8,128)(2,1)} %w_ref.2), kind=kOutput, calls=%fused_computation | convolution fusion | flops 1076363264 | bytes 4194304 | tf_op jit(solution)/shard_map/dot_general | solution.py:232
  17.1 13.0 %all-to-all-done.arrived_ref = bf16[32,32,512]{2,1,0:T(8,128)(2,1)S(1)} async-done(((bf16[32,32,512]{2,1,0:T(8,128)(2,1)}), bf16[32,32,512]{2,1,0:T(8,128)(2,1)S(1)}, u32[]{:S(2)}, u32[]{:S(2)}) %all-to-all-start) | async-done | bytes 1048608 | tf_op jit(solution)/shard_map/all_to_all | solution.py:214
  30.0 4.1 %all-to-all-start.1 = ((bf16[32,32,512]{2,1,0:T(8,128)(2,1)}), bf16[32,32,512]{2,1,0:T(8,128)(2,1)S(1)}, u32[]{:S(2)}, u32[]{:S(2)}) async-start(bf16[32,32,512]{2,1,0:T(8,128)(2,1)} %bitcast.6), calls=%async_computation.1 | async-start | bytes 2097152 | tf_op jit(solution)/shard_map/all_to_all | solution.py:214
  37.6 2.4 %collective-permute-start.1 = (bf16[8,32,512]{2,1,0:T(8,128)(2,1)S(1)}, bf16[8,32,512]{2,1,0:T(8,128)(2,1)S(1)}, u32[]{:S(2)}, u32[]{:S(2)}) collective-permute-start(bf16[8,32,512]{2,1,0:T(8,128)(2,1)S(1)} %get-tuple-element.29.refs_1_), channel_id=1, source_target_pairs={{0,1},{1,2},{2,3},{3,0},{4,5},{5,6},{6,7},{7,4},{8,9},{9,10},{10,1... | collective-permute-start | bytes 786440 | tf_op jit(solution)/shard_map/ppermute | solution.py:210
  40.0 3.9 %collective-permute-done.refs_2_ = bf16[8,32,512]{2,1,0:T(8,128)(2,1)S(1)} collective-permute-done((bf16[8,32,512]{2,1,0:T(8,128)(2,1)S(1)}, bf16[8,32,512]{2,1,0:T(8,128)(2,1)S(1)}, u32[]{:S(2)}, u32[]{:S(2)}) %collective-permute-start) | collective-permute-done | bytes 262176 | tf_op jit(solution)/shard_map/ppermute | solution.py:210
  43.9 1.7 %collective-permute-start.4 = (bf16[8,32,512]{2,1,0:T(8,128)(2,1)S(1)}, bf16[8,32,512]{2,1,0:T(8,128)(2,1)}, u32[]{:S(2)}, u32[]{:S(2)}) collective-permute-start(bf16[8,32,512]{2,1,0:T(8,128)(2,1)S(1)} %collective-permute-done.refs_2_), channel_id=1, source_target_pairs={{0,1},{1,2},{2,3},{3,0},{4,5},{5,6},{6,7},{7,4},{8,9},{9,10},{10,1... | collective-permute-start | bytes 786440 | tf_op jit(solution)/shard_map/ppermute | solution.py:210
  46.0 5.5 %all-to-all-done.1.arrived_ref = bf16[32,32,512]{2,1,0:T(8,128)(2,1)S(1)} async-done(((bf16[32,32,512]{2,1,0:T(8,128)(2,1)}), bf16[32,32,512]{2,1,0:T(8,128)(2,1)S(1)}, u32[]{:S(2)}, u32[]{:S(2)}) %all-to-all-start.1) | async-done | bytes 1048608 | tf_op jit(solution)/shard_map/all_to_all | solution.py:214
  52.6 1.5 %collective-permute-start.13 = (bf16[8,32,512]{2,1,0:T(8,128)(2,1)S(1)}, bf16[8,32,512]{2,1,0:T(8,128)(2,1)S(1)}, u32[]{:S(2)}, u32[]{:S(2)}) collective-permute-start(bf16[8,32,512]{2,1,0:T(8,128)(2,1)S(1)} %get-tuple-element.39.refs_1_), channel_id=1, source_target_pairs={{0,3},{1,0},{2,1},{3,2},{4,7},{5,4},{6,5},{7,6},{8,11},{9,8},{10,9... | collective-permute-start | bytes 786440 | tf_op jit(solution)/shard_map/ppermute | solution.py:210
  55.0 2.4 %collective-permute-start.11 = (bf16[8,32,512]{2,1,0:T(8,128)(2,1)S(1)}, bf16[8,32,512]{2,1,0:T(8,128)(2,1)S(1)}, u32[]{:S(2)}, u32[]{:S(2)}) collective-permute-start(bf16[8,32,512]{2,1,0:T(8,128)(2,1)S(1)} %get-tuple-element.39.refs_1_), channel_id=1, source_target_pairs={{0,1},{1,2},{2,3},{3,0},{4,5},{5,6},{6,7},{7,4},{8,9},{9,10},{10,1... | collective-permute-start | bytes 786440 | tf_op jit(solution)/shard_map/ppermute | solution.py:210
  57.4 6.0 %attend.2 = (bf16[8,32,512]{2,1,0:T(8,128)(2,1)S(1)}, bf16[8,32,512]{2,1,0:T(8,128)(2,1)S(1)}, bf16[2,8,32,512]{3,2,1,0:T(8,128)(2,1)S(1)}, bf16[2,8,32,512]{3,2...) custom-call(s32[16]{0:T(128)S(1)} %copy-done.1, s32[1]{0:T(128)} %bitcast.1.rank_ref, ...), custom_call_target="tpu_custom_call" | custom-call | tf_op jit(solution)/shard_map/attend/pallas_call | solution.py:98
  63.9 1.5 %collective-permute-start.15 = (bf16[8,32,512]{2,1,0:T(8,128)(2,1)S(1)}, bf16[8,32,512]{2,1,0:T(8,128)(2,1)S(1)}, u32[]{:S(2)}, u32[]{:S(2)}) collective-permute-start(bf16[8,32,512]{2,1,0:T(8,128)(2,1)S(1)} %collective-permute-done.13.refs_5_), channel_id=1, source_target_pairs={{0,3},{1,0},{2,1},{3,2},{4,7},{5,4},{6,5},{7,6},{8,11},{9,8},{10,9... | collective-permute-start | bytes 786440 | tf_op jit(solution)/shard_map/ppermute | solution.py:210
  65.5 1.7 %collective-permute-start.6 = (bf16[2,8,32,512]{3,2,1,0:T(8,128)(2,1)S(1)}, bf16[2,8,32,512]{3,2,1,0:T(8,128)(2,1)S(1)}, u32[]{:S(2)}, u32[]{:S(2)}) collective-permute-start(bf16[2,8,32,512]{3,2,1,0:T(8,128)(2,1)S(1)} %get-tuple-element.32), channel_id=1, source_target_pairs={{0,1},{1,2},{2,3},{3,0},{4,5},{5,6},{6,7},{7,4},{8,9},{9,10},{10,1... | collective-permute-start | bytes 1572872 | tf_op jit(solution)/shard_map/ppermute | solution.py:210
  68.7 4.0 %collective-permute-done.14.refs_6_ = bf16[8,32,512]{2,1,0:T(8,128)(2,1)S(1)} collective-permute-done((bf16[8,32,512]{2,1,0:T(8,128)(2,1)S(1)}, bf16[8,32,512]{2,1,0:T(8,128)(2,1)S(1)}, u32[]{:S(2)}, u32[]{:S(2)}) %collective-permute-start.14) | collective-permute-done | bytes 262176 | tf_op jit(solution)/shard_map/ppermute | solution.py:210
  72.7 1.7 %collective-permute-done.15.refs_7_ = bf16[8,32,512]{2,1,0:T(8,128)(2,1)S(1)} collective-permute-done((bf16[8,32,512]{2,1,0:T(8,128)(2,1)S(1)}, bf16[8,32,512]{2,1,0:T(8,128)(2,1)S(1)}, u32[]{:S(2)}, u32[]{:S(2)}) %collective-permute-start.15) | collective-permute-done | bytes 262176 | tf_op jit(solution)/shard_map/ppermute | solution.py:210
  74.4 5.9 %attend.3 = (bf16[8,32,512]{2,1,0:T(8,128)(2,1)S(1)}, bf16[8,32,512]{2,1,0:T(8,128)(2,1)S(1)}, bf16[2,8,32,512]{3,2,1,0:T(8,128)(2,1)S(1)}, bf16[2,8,32,512]{3,2...) custom-call(s32[16]{0:T(128)S(1)} %copy-done.1, s32[1]{0:T(128)} %bitcast.1.rank_ref, ...), custom_call_target="tpu_custom_call" | custom-call | tf_op jit(solution)/shard_map/attend/pallas_call | solution.py:98
  80.4 1.9 %collective-permute-start.17 = (bf16[2,8,32,512]{3,2,1,0:T(8,128)(2,1)S(1)}, bf16[2,8,32,512]{3,2,1,0:T(8,128)(2,1)S(1)}, u32[]{:S(2)}, u32[]{:S(2)}) collective-permute-start(bf16[2,8,32,512]{3,2,1,0:T(8,128)(2,1)S(1)} %get-tuple-element.45), channel_id=1, source_target_pairs={{0,3},{1,0},{2,1},{3,2},{4,7},{5,4},{6,5},{7,6},{8,11},{9,8},{10,9... | collective-permute-start | bytes 1572872 | tf_op jit(solution)/shard_map/ppermute | solution.py:210
  82.4 1.6 %collective-permute-done.6.from_left_ref.refs_2_ = bf16[2,8,32,512]{3,2,1,0:T(8,128)(2,1)S(1)} collective-permute-done((bf16[2,8,32,512]{3,2,1,0:T(8,128)(2,1)S(1)}, bf16[2,8,32,512]{3,2,1,0:T(8,128)(2,1)S(1)}, u32[]{:S(2)}, u32[]{:S(2)}) %collective-permute-start.6) | collective-permute-done | bytes 524320 | tf_op jit(solution)/shard_map/ppermute | solution.py:210
  83.9 1.7 %collective-permute-done.7.from_right_ref.refs_3_ = bf16[2,8,32,512]{3,2,1,0:T(8,128)(2,1)S(1)} collective-permute-done((bf16[2,8,32,512]{3,2,1,0:T(8,128)(2,1)S(1)}, bf16[2,8,32,512]{3,2,1,0:T(8,128)(2,1)S(1)}, u32[]{:S(2)}, u32[]{:S(2)}) %collective-permute-start.7) | collective-permute-done | bytes 524320 | tf_op jit(solution)/shard_map/ppermute | solution.py:210
  85.9 1.9 %collective-permute-start.9 = (bf16[8,32,512]{2,1,0:T(8,128)(2,1)S(1)}, bf16[8,32,512]{2,1,0:T(8,128)(2,1)S(1)}, u32[]{:S(2)}, u32[]{:S(2)}) collective-permute-start(bf16[8,32,512]{2,1,0:T(8,128)(2,1)S(1)} %get-tuple-element.37), channel_id=1, source_target_pairs={{0,3},{1,0},{2,1},{3,2},{4,7},{5,4},{6,5},{7,6},{8,11},{9,8},{10,9... | collective-permute-start | bytes 786440 | tf_op jit(solution)/shard_map/ppermute | solution.py:210
  87.9 7.3 %collective-permute-done.16.from_left_ref.refs_8_ = bf16[2,8,32,512]{3,2,1,0:T(8,128)(2,1)S(1)} collective-permute-done((bf16[2,8,32,512]{3,2,1,0:T(8,128)(2,1)S(1)}, bf16[2,8,32,512]{3,2,1,0:T(8,128)(2,1)S(1)}, u32[]{:S(2)}, u32[]{:S(2)}) %collective-permute-start.16) | collective-permute-done | bytes 524320 | tf_op jit(solution)/shard_map/ppermute | solution.py:210
  95.2 1.7 %collective-permute-done.17.from_right_ref.refs_9_ = bf16[2,8,32,512]{3,2,1,0:T(8,128)(2,1)S(1)} collective-permute-done((bf16[2,8,32,512]{3,2,1,0:T(8,128)(2,1)S(1)}, bf16[2,8,32,512]{3,2,1,0:T(8,128)(2,1)S(1)}, u32[]{:S(2)}, u32[]{:S(2)}) %collective-permute-start.17) | collective-permute-done | bytes 524320 | tf_op jit(solution)/shard_map/ppermute | solution.py:210
  97.2 1.9 %collective-permute-start.19 = (bf16[8,32,512]{2,1,0:T(8,128)(2,1)S(1)}, bf16[8,32,512]{2,1,0:T(8,128)(2,1)S(1)}, u32[]{:S(2)}, u32[]{:S(2)}) collective-permute-start(bf16[8,32,512]{2,1,0:T(8,128)(2,1)S(1)} %get-tuple-element.49), channel_id=1, source_target_pairs={{0,3},{1,0},{2,1},{3,2},{4,7},{5,4},{6,5},{7,6},{8,11},{9,8},{10,9... | collective-permute-start | bytes 786440 | tf_op jit(solution)/shard_map/ppermute | solution.py:210
  99.1 1.7 %collective-permute-done.8.refs_4_ = bf16[8,32,512]{2,1,0:T(8,128)(2,1)S(1)} collective-permute-done((bf16[8,32,512]{2,1,0:T(8,128)(2,1)S(1)}, bf16[8,32,512]{2,1,0:T(8,128)(2,1)S(1)}, u32[]{:S(2)}, u32[]{:S(2)}) %collective-permute-start.8) | collective-permute-done | bytes 262176 | tf_op jit(solution)/shard_map/ppermute | solution.py:210
  100.8 1.7 %collective-permute-done.9.refs_5_ = bf16[8,32,512]{2,1,0:T(8,128)(2,1)S(1)} collective-permute-done((bf16[8,32,512]{2,1,0:T(8,128)(2,1)S(1)}, bf16[8,32,512]{2,1,0:T(8,128)(2,1)S(1)}, u32[]{:S(2)}, u32[]{:S(2)}) %collective-permute-start.9) | collective-permute-done | bytes 262176 | tf_op jit(solution)/shard_map/ppermute | solution.py:210
  102.5 2.9 %collective-permute-done.18.refs_10_ = bf16[8,32,512]{2,1,0:T(8,128)(2,1)S(1)} collective-permute-done((bf16[8,32,512]{2,1,0:T(8,128)(2,1)S(1)}, bf16[8,32,512]{2,1,0:T(8,128)(2,1)S(1)}, u32[]{:S(2)}, u32[]{:S(2)}) %collective-permute-start.18) | collective-permute-done | bytes 262176 | tf_op jit(solution)/shard_map/ppermute | solution.py:210
  106.8 3.0 %place.1 = bf16[32,32,1024]{2,1,0:T(8,128)(2,1)} custom-call(s32[16]{0:T(128)S(1)} %bitcast.13, bf16[8,32,512]{2,1,0:T(8,128)(2,1)S(1)} %get-tuple-element.30.refs_0_, bf16[8,32,512]{2,1,0:T(8,128)(2,1)S(1)} %get-tuple-element.31.refs_1_, bf16[2,8,32,512]{3,2,1,0:T(8,128)(2,1)S(1)} %collective-permute-done.6.from_left_ref.refs_2_, ...), custom_call_target="tpu_custom_call" | custom-call | tf_op jit(solution)/shard_map/place/pallas_call | solution.py:154
  109.8 7.1 %all-to-all-start.2 = ((bf16[32,32,1024]{2,1,0:T(8,128)(2,1)}), bf16[32,32,1024]{2,1,0:T(8,128)(2,1)}, u32[]{:S(2)}, u32[]{:S(2)}) async-start(bf16[32,32,1024]{2,1,0:T(8,128)(2,1)} %place.1), calls=%async_computation.2 | async-start | bytes 4194304 | tf_op jit(solution)/shard_map/all_to_all | solution.py:214
  116.9 6.1 %project.1.gate_ref = bf16[1024,1024]{1,0:T(8,128)(2,1)} custom-call(bf16[1024,1024]{1,0:T(8,128)(2,1)} %bitcast.20, bf16[1024,2048]{1,0:T(8,128)(2,1)} %w_ref.2), custom_call_target="tpu_custom_call" | custom-call | tf_op jit(solution)/shard_map/project/pallas_call | solution.py:174
  123.0 23.8 %all-to-all-done.2 = bf16[32,32,1024]{2,1,0:T(8,128)(2,1)} async-done(((bf16[32,32,1024]{2,1,0:T(8,128)(2,1)}), bf16[32,32,1024]{2,1,0:T(8,128)(2,1)}, u32[]{:S(2)}, u32[]{:S(2)}) %all-to-all-start.2) | async-done | bytes 2097184 | tf_op jit(solution)/shard_map/all_to_all | solution.py:214
  146.9 7.0 %finish.1 = bf16[1024,1024]{1,0:T(8,128)(2,1)} custom-call(bf16[1024,1024]{1,0:T(8,128)(2,1)} %bitcast.7.normed_ref, bf16[1024,1024]{1,0:T(8,128)(2,1)} %project.1.gate_ref, bf16[1024,1024]{1,0:T(8,128)(2,1)} %bitcast.21, bf16[1024,1024]{1,0:T(8,128)(2,1)} %w_ref.3), custom_call_target="tpu_custom_call" | custom-call | tf_op jit(solution)/shard_map/finish/pallas_call | solution.py:197
  (29 shorter events, 10.1 us)
Async XLA Ops:
  4.4 25.7 %all-to-all-start = ((bf16[32,32,512]{2,1,0:T(8,128)(2,1)}), bf16[32,32,512]{2,1,0:T(8,128)(2,1)S(1)}, u32[]{:S(2)}, u32[]{:S(2)}) async-start(bf16[32,32,512]{2,1,0:T(8,128)(2,1)} %bitcast.3), calls=%async_computation | async-start | bytes 2097152 | tf_op jit(solution)/shard_map/all_to_all | solution.py:214
  17.1 17.0 %copy-start = (s32[16,1]{0,1:T(1,128)S(1)}, s32[16,1]{0,1:T(1,128)}, u32[]{:S(2)}) copy-start(s32[16,1]{0,1:T(1,128)} %param.10) | copy-start | bytes 196
  30.0 27.3 %copy-start.1 = (s32[16]{0:T(128)S(1)}, s32[16]{0:T(128)}, u32[]{:S(2)}) copy-start(s32[16]{0:T(128)} %lengths_ref.3) | copy-start | bytes 196
  30.0 21.4 %all-to-all-start.1 = ((bf16[32,32,512]{2,1,0:T(8,128)(2,1)}), bf16[32,32,512]{2,1,0:T(8,128)(2,1)S(1)}, u32[]{:S(2)}, u32[]{:S(2)}) async-start(bf16[32,32,512]{2,1,0:T(8,128)(2,1)} %bitcast.6), calls=%async_computation.1 | async-start | bytes 2097152 | tf_op jit(solution)/shard_map/all_to_all | solution.py:214
  34.7 9.2 %collective-permute-start = (bf16[8,32,512]{2,1,0:T(8,128)(2,1)S(1)}, bf16[8,32,512]{2,1,0:T(8,128)(2,1)S(1)}, u32[]{:S(2)}, u32[]{:S(2)}) collective-permute-start(bf16[8,32,512]{2,1,0:T(8,128)(2,1)S(1)} %get-tuple-element.28.refs_0_), channel_id=1, source_target_pairs={{0,1},{1,2},{2,3},{3,0},{4,5},{5,6},{6,7},{7,4},{8,9},{9,10},{10,1... | collective-permute-start | bytes 786440 | tf_op jit(solution)/shard_map/ppermute | solution.py:210
  35.3 10.4 %collective-permute-start.3 = (bf16[8,32,512]{2,1,0:T(8,128)(2,1)S(1)}, bf16[8,32,512]{2,1,0:T(8,128)(2,1)S(1)}, u32[]{:S(2)}, u32[]{:S(2)}) collective-permute-start(bf16[8,32,512]{2,1,0:T(8,128)(2,1)S(1)} %get-tuple-element.29.refs_1_), channel_id=1, source_target_pairs={{0,3},{1,0},{2,1},{3,2},{4,7},{5,4},{6,5},{7,6},{8,11},{9,8},{10,9... | collective-permute-start | bytes 786440 | tf_op jit(solution)/shard_map/ppermute | solution.py:210
  36.8 15.8 %collective-permute-start.2 = (bf16[8,32,512]{2,1,0:T(8,128)(2,1)S(1)}, bf16[8,32,512]{2,1,0:T(8,128)(2,1)S(1)}, u32[]{:S(2)}, u32[]{:S(2)}) collective-permute-start(bf16[8,32,512]{2,1,0:T(8,128)(2,1)S(1)} %get-tuple-element.28.refs_0_), channel_id=1, source_target_pairs={{0,3},{1,0},{2,1},{3,2},{4,7},{5,4},{6,5},{7,6},{8,11},{9,8},{10,9... | collective-permute-start | bytes 786440 | tf_op jit(solution)/shard_map/ppermute | solution.py:210
  37.6 16.5 %collective-permute-start.1 = (bf16[8,32,512]{2,1,0:T(8,128)(2,1)S(1)}, bf16[8,32,512]{2,1,0:T(8,128)(2,1)S(1)}, u32[]{:S(2)}, u32[]{:S(2)}) collective-permute-start(bf16[8,32,512]{2,1,0:T(8,128)(2,1)S(1)} %get-tuple-element.29.refs_1_), channel_id=1, source_target_pairs={{0,1},{1,2},{2,3},{3,0},{4,5},{5,6},{6,7},{7,4},{8,9},{9,10},{10,1... | collective-permute-start | bytes 786440 | tf_op jit(solution)/shard_map/ppermute | solution.py:210
  43.9 11.1 %collective-permute-start.4 = (bf16[8,32,512]{2,1,0:T(8,128)(2,1)S(1)}, bf16[8,32,512]{2,1,0:T(8,128)(2,1)}, u32[]{:S(2)}, u32[]{:S(2)}) collective-permute-start(bf16[8,32,512]{2,1,0:T(8,128)(2,1)S(1)} %collective-permute-done.refs_2_), channel_id=1, source_target_pairs={{0,1},{1,2},{2,3},{3,0},{4,5},{5,6},{6,7},{7,4},{8,9},{9,10},{10,1... | collective-permute-start | bytes 786440 | tf_op jit(solution)/shard_map/ppermute | solution.py:210
  45.7 11.7 %collective-permute-start.5 = (bf16[8,32,512]{2,1,0:T(8,128)(2,1)S(1)}, bf16[8,32,512]{2,1,0:T(8,128)(2,1)}, u32[]{:S(2)}, u32[]{:S(2)}) collective-permute-start(bf16[8,32,512]{2,1,0:T(8,128)(2,1)S(1)} %collective-permute-done.3.refs_5_), channel_id=1, source_target_pairs={{0,3},{1,0},{2,1},{3,2},{4,7},{5,4},{6,5},{7,6},{8,11},{9,8},{10,9... | collective-permute-start | bytes 786440 | tf_op jit(solution)/shard_map/ppermute | solution.py:210
  52.0 11.4 %collective-permute-start.10 = (bf16[8,32,512]{2,1,0:T(8,128)(2,1)S(1)}, bf16[8,32,512]{2,1,0:T(8,128)(2,1)S(1)}, u32[]{:S(2)}, u32[]{:S(2)}) collective-permute-start(bf16[8,32,512]{2,1,0:T(8,128)(2,1)S(1)} %get-tuple-element.38.refs_0_), channel_id=1, source_target_pairs={{0,1},{1,2},{2,3},{3,0},{4,5},{5,6},{6,7},{7,4},{8,9},{9,10},{10,1... | collective-permute-start | bytes 786440 | tf_op jit(solution)/shard_map/ppermute | solution.py:210
  52.6 10.8 %collective-permute-start.13 = (bf16[8,32,512]{2,1,0:T(8,128)(2,1)S(1)}, bf16[8,32,512]{2,1,0:T(8,128)(2,1)S(1)}, u32[]{:S(2)}, u32[]{:S(2)}) collective-permute-start(bf16[8,32,512]{2,1,0:T(8,128)(2,1)S(1)} %get-tuple-element.39.refs_1_), channel_id=1, source_target_pairs={{0,3},{1,0},{2,1},{3,2},{4,7},{5,4},{6,5},{7,6},{8,11},{9,8},{10,9... | collective-permute-start | bytes 786440 | tf_op jit(solution)/shard_map/ppermute | solution.py:210
  54.1 14.2 %collective-permute-start.12 = (bf16[8,32,512]{2,1,0:T(8,128)(2,1)S(1)}, bf16[8,32,512]{2,1,0:T(8,128)(2,1)S(1)}, u32[]{:S(2)}, u32[]{:S(2)}) collective-permute-start(bf16[8,32,512]{2,1,0:T(8,128)(2,1)S(1)} %get-tuple-element.38.refs_0_), channel_id=1, source_target_pairs={{0,3},{1,0},{2,1},{3,2},{4,7},{5,4},{6,5},{7,6},{8,11},{9,8},{10,9... | collective-permute-start | bytes 786440 | tf_op jit(solution)/shard_map/ppermute | solution.py:210
  55.0 13.7 %collective-permute-start.11 = (bf16[8,32,512]{2,1,0:T(8,128)(2,1)S(1)}, bf16[8,32,512]{2,1,0:T(8,128)(2,1)S(1)}, u32[]{:S(2)}, u32[]{:S(2)}) collective-permute-start(bf16[8,32,512]{2,1,0:T(8,128)(2,1)S(1)} %get-tuple-element.39.refs_1_), channel_id=1, source_target_pairs={{0,1},{1,2},{2,3},{3,0},{4,5},{5,6},{6,7},{7,4},{8,9},{9,10},{10,1... | collective-permute-start | bytes 786440 | tf_op jit(solution)/shard_map/ppermute | solution.py:210
  63.4 9.3 %collective-permute-start.14 = (bf16[8,32,512]{2,1,0:T(8,128)(2,1)S(1)}, bf16[8,32,512]{2,1,0:T(8,128)(2,1)S(1)}, u32[]{:S(2)}, u32[]{:S(2)}) collective-permute-start(bf16[8,32,512]{2,1,0:T(8,128)(2,1)S(1)} %collective-permute-done.10.refs_2_), channel_id=1, source_target_pairs={{0,1},{1,2},{2,3},{3,0},{4,5},{5,6},{6,7},{7,4},{8,9},{9,10},{10,1... | collective-permute-start | bytes 786440 | tf_op jit(solution)/shard_map/ppermute | solution.py:210
  63.9 10.5 %collective-permute-start.15 = (bf16[8,32,512]{2,1,0:T(8,128)(2,1)S(1)}, bf16[8,32,512]{2,1,0:T(8,128)(2,1)S(1)}, u32[]{:S(2)}, u32[]{:S(2)}) collective-permute-start(bf16[8,32,512]{2,1,0:T(8,128)(2,1)S(1)} %collective-permute-done.13.refs_5_), channel_id=1, source_target_pairs={{0,3},{1,0},{2,1},{3,2},{4,7},{5,4},{6,5},{7,6},{8,11},{9,8},{10,9... | collective-permute-start | bytes 786440 | tf_op jit(solution)/shard_map/ppermute | solution.py:210
  65.5 18.5 %collective-permute-start.6 = (bf16[2,8,32,512]{3,2,1,0:T(8,128)(2,1)S(1)}, bf16[2,8,32,512]{3,2,1,0:T(8,128)(2,1)S(1)}, u32[]{:S(2)}, u32[]{:S(2)}) collective-permute-start(bf16[2,8,32,512]{3,2,1,0:T(8,128)(2,1)S(1)} %get-tuple-element.32), channel_id=1, source_target_pairs={{0,1},{1,2},{2,3},{3,0},{4,5},{5,6},{6,7},{7,4},{8,9},{9,10},{10,1... | collective-permute-start | bytes 1572872 | tf_op jit(solution)/shard_map/ppermute | solution.py:210
  68.4 17.3 %collective-permute-start.7 = (bf16[2,8,32,512]{3,2,1,0:T(8,128)(2,1)S(1)}, bf16[2,8,32,512]{3,2,1,0:T(8,128)(2,1)S(1)}, u32[]{:S(2)}, u32[]{:S(2)}) collective-permute-start(bf16[2,8,32,512]{3,2,1,0:T(8,128)(2,1)S(1)} %get-tuple-element.33), channel_id=1, source_target_pairs={{0,3},{1,0},{2,1},{3,2},{4,7},{5,4},{6,5},{7,6},{8,11},{9,8},{10,9... | collective-permute-start | bytes 1572872 | tf_op jit(solution)/shard_map/ppermute | solution.py:210
  80.3 14.9 %collective-permute-start.16 = (bf16[2,8,32,512]{3,2,1,0:T(8,128)(2,1)S(1)}, bf16[2,8,32,512]{3,2,1,0:T(8,128)(2,1)S(1)}, u32[]{:S(2)}, u32[]{:S(2)}) collective-permute-start(bf16[2,8,32,512]{3,2,1,0:T(8,128)(2,1)S(1)} %get-tuple-element.44), channel_id=1, source_target_pairs={{0,1},{1,2},{2,3},{3,0},{4,5},{5,6},{6,7},{7,4},{8,9},{9,10},{10,1... | collective-permute-start | bytes 1572872 | tf_op jit(solution)/shard_map/ppermute | solution.py:210
  80.4 16.4 %collective-permute-start.17 = (bf16[2,8,32,512]{3,2,1,0:T(8,128)(2,1)S(1)}, bf16[2,8,32,512]{3,2,1,0:T(8,128)(2,1)S(1)}, u32[]{:S(2)}, u32[]{:S(2)}) collective-permute-start(bf16[2,8,32,512]{3,2,1,0:T(8,128)(2,1)S(1)} %get-tuple-element.45), channel_id=1, source_target_pairs={{0,3},{1,0},{2,1},{3,2},{4,7},{5,4},{6,5},{7,6},{8,11},{9,8},{10,9... | collective-permute-start | bytes 1572872 | tf_op jit(solution)/shard_map/ppermute | solution.py:210
  85.8 15.0 %collective-permute-start.8 = (bf16[8,32,512]{2,1,0:T(8,128)(2,1)S(1)}, bf16[8,32,512]{2,1,0:T(8,128)(2,1)S(1)}, u32[]{:S(2)}, u32[]{:S(2)}) collective-permute-start(bf16[8,32,512]{2,1,0:T(8,128)(2,1)S(1)} %get-tuple-element.36), channel_id=1, source_target_pairs={{0,1},{1,2},{2,3},{3,0},{4,5},{5,6},{6,7},{7,4},{8,9},{9,10},{10,1... | collective-permute-start | bytes 786440 | tf_op jit(solution)/shard_map/ppermute | solution.py:210
  85.9 16.6 %collective-permute-start.9 = (bf16[8,32,512]{2,1,0:T(8,128)(2,1)S(1)}, bf16[8,32,512]{2,1,0:T(8,128)(2,1)S(1)}, u32[]{:S(2)}, u32[]{:S(2)}) collective-permute-start(bf16[8,32,512]{2,1,0:T(8,128)(2,1)S(1)} %get-tuple-element.37), channel_id=1, source_target_pairs={{0,3},{1,0},{2,1},{3,2},{4,7},{5,4},{6,5},{7,6},{8,11},{9,8},{10,9... | collective-permute-start | bytes 786440 | tf_op jit(solution)/shard_map/ppermute | solution.py:210
  97.0 8.4 %collective-permute-start.18 = (bf16[8,32,512]{2,1,0:T(8,128)(2,1)S(1)}, bf16[8,32,512]{2,1,0:T(8,128)(2,1)S(1)}, u32[]{:S(2)}, u32[]{:S(2)}) collective-permute-start(bf16[8,32,512]{2,1,0:T(8,128)(2,1)S(1)} %get-tuple-element.48), channel_id=1, source_target_pairs={{0,1},{1,2},{2,3},{3,0},{4,5},{5,6},{6,7},{7,4},{8,9},{9,10},{10,1... | collective-permute-start | bytes 786440 | tf_op jit(solution)/shard_map/ppermute | solution.py:210
  97.2 9.6 %collective-permute-start.19 = (bf16[8,32,512]{2,1,0:T(8,128)(2,1)S(1)}, bf16[8,32,512]{2,1,0:T(8,128)(2,1)S(1)}, u32[]{:S(2)}, u32[]{:S(2)}) collective-permute-start(bf16[8,32,512]{2,1,0:T(8,128)(2,1)S(1)} %get-tuple-element.49), channel_id=1, source_target_pairs={{0,3},{1,0},{2,1},{3,2},{4,7},{5,4},{6,5},{7,6},{8,11},{9,8},{10,9... | collective-permute-start | bytes 786440 | tf_op jit(solution)/shard_map/ppermute | solution.py:210
  109.8 37.0 %all-to-all-start.2 = ((bf16[32,32,1024]{2,1,0:T(8,128)(2,1)}), bf16[32,32,1024]{2,1,0:T(8,128)(2,1)}, u32[]{:S(2)}, u32[]{:S(2)}) async-start(bf16[32,32,1024]{2,1,0:T(8,128)(2,1)} %place.1), calls=%async_computation.2 | async-start | bytes 4194304 | tf_op jit(solution)/shard_map/all_to_all | solution.py:214
